TPU v7x, 512 devices: a whole 4x8x8 slice. The times are simulated.
512 devices in a mesh: run: 16 (over y, x_lo), fsdp: 32 (over x_hi, z, core).
Axes of the slice: x: 4 (x_hi: 2, x_lo: 2; x = x_hi * 2 + x_lo), y: 8, z: 8, core: 2. Of those that a mesh axis runs over, the one named last changes fastest.
Arguments:
- table: bfloat16 [256, 4608], P('fsdp', 'run'), may hold values from -6 to 6
- token_ids: int32 [4, 128], P(None, 'fsdp'), may hold values from 0 to 255
- cotangent: bfloat16 [4, 128, 4608], P(None, 'fsdp', 'run'), may hold values from -6 to 6
- gate_weight: bfloat16 [4, 4608, 18432], P(None, 'run', 'fsdp'), may hold values from -6 to 6
- up_weight: bfloat16 [4, 4608, 18432], P(None, 'run', 'fsdp'), may hold values from -6 to 6
- down_weight: bfloat16 [4, 4608, 18432], P(None, 'run', 'fsdp'), may hold values from -6 to 6
Outputs:
- merged_gate: bfloat16 [4608, 18432], P('run', 'fsdp')
- merged_up: bfloat16 [4608, 18432], P('run', 'fsdp')
- merged_down: bfloat16 [4608, 18432], P('run', 'fsdp')
All inputs are finite; a program needn't handle non-finite values.
Results may differ from a plain program's by a relative error of at most 0.039.
Values may be sent and summed in bfloat16 or wider, within the bound.
A program may use at most 64 MiB of HBM per device.

v0:
```python
import jax
import jax.numpy as jnp
from jax import lax
from jax.sharding import PartitionSpec as P

D = 4608
FF = 18432


PRIOR = 0.01


def gelu_tanh(value):
    return jax.nn.gelu(value, approximate=True)


def local_grads(gate, up, back):
    act, slope = jax.jvp(gelu_tanh, (gate,), (jnp.ones_like(gate),))
    hidden = (act * up).astype(jnp.bfloat16)
    d_gate = (back * up * slope).astype(jnp.bfloat16)
    d_up = (back * act).astype(jnp.bfloat16)
    return (hidden, d_gate, d_up)


def merge_runs(weights, fisher):
    factor = fisher.astype(jnp.float32) + PRIOR
    numer = jnp.sum(factor * weights.astype(jnp.float32), axis=0)
    denom = jnp.sum(factor, axis=0)
    return (numer / denom).astype(jnp.bfloat16)


def on_device(table, token_ids, cotangent, gate_weight, up_weight, down_weight):
    entries, ids_all, cot_all = (
        lax.all_gather(table, "fsdp", axis=0, tiled=True),
        lax.all_gather(token_ids, "fsdp", axis=1, tiled=True),
        lax.all_gather(cotangent, "fsdp", axis=1, tiled=True),
    )
    run_count, tok_count = ids_all.shape
    tok_rows = jnp.take(entries, ids_all.reshape(-1), axis=0).reshape(run_count, tok_count, -1)
    gate_part = jnp.einsum(
        "rtd,rdf->rtf", tok_rows, gate_weight, preferred_element_type=jnp.float32
    ) * D ** (-0.5)
    up_part = jnp.einsum(
        "rtd,rdf->rtf", tok_rows, up_weight, preferred_element_type=jnp.float32
    ) * D ** (-0.5)
    back_part = jnp.einsum(
        "rtd,rdf->rtf", cot_all, down_weight, preferred_element_type=jnp.float32
    ) * FF ** (-0.5)
    gate_full, up_full, back_full = (
        lax.psum(gate_part.astype(jnp.bfloat16), "run").astype(jnp.float32),
        lax.psum(up_part.astype(jnp.bfloat16), "run").astype(jnp.float32),
        lax.psum(back_part.astype(jnp.bfloat16), "run").astype(jnp.float32),
    )
    hidden, d_gate, d_up = local_grads(gate_full, up_full, back_full)
    grad_gate = jnp.einsum(
        "rtd,rtf->rdf", tok_rows, d_gate, preferred_element_type=jnp.float32
    ) * D ** (-0.5)
    grad_up = jnp.einsum(
        "rtd,rtf->rdf", tok_rows, d_up, preferred_element_type=jnp.float32
    ) * D ** (-0.5)
    grad_down = jnp.einsum(
        "rtd,rtf->rdf", cot_all, hidden, preferred_element_type=jnp.float32
    ) * FF ** (-0.5)
    fisher_gate = (grad_gate * grad_gate).astype(jnp.bfloat16)
    fisher_up = (grad_up * grad_up).astype(jnp.bfloat16)
    fisher_down = (grad_down * grad_down).astype(jnp.bfloat16)
    return (
        merge_runs(gate_weight, fisher_gate),
        merge_runs(up_weight, fisher_up),
        merge_runs(down_weight, fisher_down),
    )


def solution(mesh):
    return jax.shard_map(
        on_device,
        mesh=mesh,
        in_specs=(
            P("fsdp", "run"),
            P(None, "fsdp"),
            P(None, "fsdp", "run"),
            P(None, "run", "fsdp"),
            P(None, "run", "fsdp"),
            P(None, "run", "fsdp"),
        ),
        out_specs=(P("run", "fsdp"), P("run", "fsdp"), P("run", "fsdp")),
        check_vma=False,
    )
```

profile of v0, /device:TPU:6, one launch (start us, length us, event | category | flops | bytes accessed | tf_op | source)
XLA Modules:
  0.0 299.0 jit_solution(3075118976226613194)
XLA Ops:
  7.2 0.0 all-reduce.3.cloned.1.call-start
  7.2 47.0 %all_gather.10 = bf16[256,288]{1,0:T(8,128)(2,1)S(1)} all-gather(bf16[8,288]{1,0:T(8,128)(2,1)} %param.6), channel_id=1, replica_groups=mesh['run'=16,'fsdp'=32] {'fsdp'}, dimensions={0}, use_global_device_ids=true | all-gather | bytes 152064 | tf_op jit(solution)/shard_map/all_gather | solution.py:34
  54.2 0.8 copy.15
  55.0 36.9 %all-gather = s32[32,4,4]{2,1,0:T(4,128)S(1)} all-gather(s32[1,4,4]{2,1,0:T(4,128)S(1)} %bitcast.23), channel_id=1, replica_groups=mesh['run'=16,'fsdp'=32] {'fsdp'}, dimensions={0}, use_global_device_ids=true | all-gather | bytes 2112 | tf_op jit(solution)/shard_map/all_gather | solution.py:35
  91.9 0.1 copy.16
  92.0 0.0 copy-start.5
  92.0 0.0 copy-start.3
  92.0 1.9 gather_fusion
  93.9 0.2 copy.17
  94.2 0.0 copy-done.5
  94.2 39.1 %all_gather.11 = bf16[4,128,288]{2,0,1:T(4,128)(2,1)S(1)} all-gather(bf16[4,4,288]{2,0,1:T(4,128)(2,1)S(1)} %copy.18), channel_id=1, replica_groups=mesh['run'=16,'fsdp'=32] {'fsdp'}, dimensions={1}, use_global_device_ids=true | all-gather | bytes 304128 | tf_op jit(solution)/shard_map/all_gather | solution.py:36
  133.3 1.6 fusion.5
  134.9 1.6 fusion.6
  136.5 1.6 fusion.4
  138.1 0.0 all-reduce.3.cloned.1.call-update
  138.1 146.1 %all-reduce.3.cloned.1.call-done = (bf16[4,128,576]{1,2,0:T(8,128)(2,1)}, bf16[4,128,576]{1,2,0:T(8,128)(2,1)}, bf16[4,128,576]{1,2,0:T(8,128)(2,1)}) async-done(((bf16[4,128,576]{1,2,0:T(8,128)(2,1)}, bf16[4,128,576]{1,2,0:T(8,128)(2,1)}, bf16[4,128,576]{1,2,0:T(8,128)(2,1)}), (bf16[4,128,576]{1,2,0:T(8,128)(2,1)}, bf16[4,128,576]{1,2,0:T(8,128)(2,1)}, ...) | async-done | bytes 1769488 | tf_op jit(solution)/shard_map/psum | solution.py:51
  284.2 2.9 bitcast_reduce_fusion
  287.1 0.0 copy-done.2
  287.1 0.0 copy-done.6
  287.1 0.0 copy-start.4
  287.2 1.7 fusion.2
  288.9 1.3 fusion.1
  290.2 0.8 divide_convert_fusion.2
  291.0 1.1 divide_convert_fusion
  (16 shorter events, 0.1 us)
Async XLA Ops:
  7.2 277.0 %all-reduce.3.cloned.1.call-start = ((), (), s32[]{:S(2)}) async-start(), calls=%async_computation | async-start | bytes 3538944 | tf_op jit(solution)/shard_map/psum | solution.py:51
  92.0 2.2 copy-start.5
  92.0 41.3 %copy-start.3 = (bf16[4,288,576]{2,1,0:T(8,128)(2,1)S(1)}, bf16[4,288,576]{2,1,0:T(8,128)(2,1)}, u32[]{:S(2)}) copy-start(bf16[4,288,576]{2,1,0:T(8,128)(2,1)} %param.10) | copy-start | bytes 3981316
  133.3 1.6 copy-start.1
  134.9 1.6 copy-start
  284.2 2.9 copy-start.2
  284.2 2.9 copy-start.6
  284.2 2.9 copy-start.7
  284.2 2.9 copy-start.8
  287.1 1.7 copy-start.4
Sparse Core Ops, SparseCore 0:
  138.2 145.9 all-reduce.2
where the time goes:
time: 299 us
  waiting for transfers between devices  146 us (49%)
  blocking collectives  123 us (41%)
  between operations  14.2 us (5%)
  matrix products  10.7 us (4%)
  local copies, waits for them, and re-layouts  3.03 us (1%)
    psum x1, waiting for transfers between devices, on_device(): lax.psum(up_part.astype(jnp.bfloat16), 'run').astype(jnp.float32)  146 us
    all_gather x1, blocking collectives, on_device(): lax.all_gather(table, 'fsdp', axis=0, tiled=True)  47 us
    all_gather x1, blocking collectives, on_device(): lax.all_gather(cotangent, 'fsdp', axis=1, tiled=True)  39.1 us
    all_gather x1, blocking collectives, on_device(): lax.all_gather(token_ids, 'fsdp', axis=1, tiled=True)  36.9 us
  transfers between devices with their start and end apart: 1, of which 1 were waited for; matrix products, arithmetic and copies ran while one was open for 0% of the time, Pallas kernels for 0%

commit v1 on v0

v1 whole, which is shorter than its diff:
```python
import jax
import jax.numpy as jnp
from jax import lax
from jax.experimental import pallas as pl
from jax.experimental.pallas import tpu as pltpu
from jax.sharding import PartitionSpec as P

D = 4608
FF = 18432
PRIOR = 0.01
DB = 288
FB = 576
RUNS = 4
TOK = 128
NY = 8
MESH = pl.DeviceIdType.MESH
BF = jnp.bfloat16
F32 = jnp.float32
WIDTH = (768, 1024)
ORDER = (4, 3, 5, 2, 6, 1, 7)


def dot(a, b):
    return jnp.dot(a, b, preferred_element_type=F32)


def iota(shape, dim):
    return lax.broadcasted_iota(jnp.int32, shape, dim)


def place(rows, shift):
    return (iota((rows, 128), 1) == iota((rows, 128), 0) + shift).astype(BF)


def kernel(
    ids_ref, table_ref, cot_ref, wg_hbm, wu_hbm, wd_hbm,
    og_ref, ou_ref, od_ref,
    wg, wu, wd, wt, m1, m2, rows_s, cot_s, rows_t, cot_t, tbl,
    sx0, sx1, rx0, rx1, own0, own1, sy0, sy1, ry0, ry1, h0, h1,
    num_g, num_u, num_d, num_t, den_g, den_u, den_d, den_t,
    w_sem, g_send, g_recv, f_send, f_recv,
    x_send, x_recv, y_send, y_recv, ay_send, ay_recv, ax_send, ax_recv,
):
    sx, rx, own, sy, ry, hb = (sx0, sx1), (rx0, rx1), (own0, own1), (sy0, sy1), (ry0, ry1), (h0, h1)
    run, fs = lax.axis_index("run"), lax.axis_index("fsdp")
    y, xl = run // 2, run % 2
    chip, core = fs // 2, fs % 2
    xh, z = chip // 8, chip % 8

    def y_peer(k):
        return (lax.rem(y + k, NY) * 2 + xl, fs)

    x_peer = (y * 2 + 1 - xl, fs)
    sibling = (run, chip * 2 + 1 - core)
    gather_peers = []
    for dz in (4, 3, 5, 2, 6, 1, 7, 0):
        for dx in (1, 0):
            if dz or dx:
                other = lax.rem(xh + dx, 2) * 8 + lax.rem(z + dz, 8)
                gather_peers.append((run, other * 2 + core))

    barrier = pltpu.get_barrier_semaphore()
    everyone = gather_peers + [sibling, x_peer] + [y_peer(k) for k in ORDER]
    for peer in everyone:
        pl.semaphore_signal(barrier, inc=1, device_id=peer, device_id_type=MESH)

    weight_copies = []
    for i, (src, dst) in enumerate(((wg_hbm, wg), (wu_hbm, wu), (wd_hbm, wd))):
        copy = pltpu.make_async_copy(src, dst, w_sem.at[i])
        copy.start()
        weight_copies.append(copy)

    table = table_ref[...].astype(F32)
    cot = jnp.concatenate([cot_ref[r].astype(F32) for r in range(RUNS)], axis=0)
    ids = jnp.zeros((16, 128), F32)
    row, lane = iota((16, 128), 0), iota((16, 128), 1)
    for r in range(RUNS):
        for t in range(4):
            ids = jnp.where((row == 4 * r + t) & (lane == 64), ids_ref[r, t].astype(F32), ids)
    tail = dot(cot[:, 256:288].astype(BF), place(32, 32))
    table_tail = dot(table[:, 256:288].astype(BF), place(32, 0))
    tail = tail + ids + jnp.concatenate([table_tail, jnp.zeros((8, 128), F32)], axis=0)
    folded = jnp.concatenate([table[:, 0:128], table[:, 128:256]], axis=0)
    m1[core, chip] = jnp.concatenate([folded, tail], axis=1).astype(BF)
    m2[core, chip] = cot[:, 0:256].astype(BF)

    pl.semaphore_wait(barrier, len(everyone))

    sends = []

    def send(src, dst, s_sem, r_sem, peer):
        copy = pltpu.make_async_remote_copy(
            src_ref=src, dst_ref=dst, send_sem=s_sem, recv_sem=r_sem, device_id=peer, device_id_type=MESH
        )
        copy.start()
        sends.append(copy)
        return copy

    gathers = []
    for j, buf in enumerate((m1, m2)):
        gathers.append([
            send(buf.at[core, chip], buf.at[core, chip], g_send.at[j, i], g_recv.at[j, i], peer)
            for i, peer in enumerate(gather_peers)
        ])

    for copy in weight_copies:
        copy.wait()
    for r in range(RUNS):
        wt[r] = jnp.concatenate([wg[r, :, 512:576], wu[r, :, 512:576]], axis=1)

    def finish_gather(j, buf):
        for copy in gathers[j]:
            copy.wait_recv()
        fwd = send(buf.at[core], buf.at[core], f_send.at[j], f_recv.at[j], sibling)
        fwd.wait_recv()

    def picker(r):
        i, g = iota((TOK, 512), 0), iota((TOK, 512), 1)
        return (g == 16 * (i // 4) + 4 * r + i % 4).astype(BF)

    finish_gather(0, m1)
    m1f = m1[...].astype(F32).reshape(32, 16, 256)
    tbl[:, 0:128] = m1f[:, 0:8, 0:128].reshape(256, 128).astype(BF)
    tbl[:, 128:256] = m1f[:, 8:16, 0:128].reshape(256, 128).astype(BF)
    tbl[:, 256:384] = m1f[:, 0:8, 128:256].reshape(256, 128).astype(BF)

    def pick_rows(r):
        z_tail = dot(picker(r), m1[...].reshape(512, 256)[:, 128:256])
        j = iota((TOK, 256), 1)
        entry = ((j % 128) // 8) * 16 + (j // 128) * 8 + j % 8
        hot = (z_tail[:, 64:65].astype(jnp.int32) == entry).astype(BF)
        rows = dot(hot, tbl[...])
        rows_s[r] = rows.astype(BF)
        rows_t[r] = rows.T.astype(BF)
        cot_tail = pltpu.roll(z_tail, 96, 1)
        cot_s[r, :, 256:384] = cot_tail.astype(BF)
        cot_t[r, 256:384, :] = cot_tail.T.astype(BF)

    def pick_cot(r):
        main = dot(picker(r), m2[...].reshape(512, 256))
        cot_s[r, :, 0:256] = main.astype(BF)
        cot_t[r, 0:256, :] = main.T.astype(BF)

    def forward_gu(r, h, out):
        rows = rows_s[r, :, 0:DB]
        cols = slice(256 * h, 256 * h + 256)
        out[:, 0:256] = (dot(rows, wg[r, :, cols]) * D ** -0.5).astype(out.dtype)
        out[:, 256:512] = (dot(rows, wu[r, :, cols]) * D ** -0.5).astype(out.dtype)
        if h == 1:
            out[:, 768:896] = (dot(rows, wt[r]) * D ** -0.5).astype(out.dtype)

    def forward_b(r, h, out):
        cots = cot_s[r, :, 0:DB]
        out[:, 512:768] = (dot(cots, wd[r, :, 256 * h:256 * h + 256]) * FF ** -0.5).astype(out.dtype)
        if h == 1:
            last = dot(cots, wd[r, :, 512:576]) * FF ** -0.5
            out[:, 896:1024] = jnp.concatenate([last, jnp.zeros_like(last)], axis=1).astype(out.dtype)

    def start_x(p, h):
        return send(sx[h].at[p], rx[h].at[p], x_send.at[p, h], x_recv.at[p, h], x_peer)

    exchanges = {}
    theirs, mine = (1 - xl, 3 - xl), (xl, 2 + xl)
    pick_rows(theirs[0])
    forward_gu(theirs[0], 0, sx[0].at[0])
    finish_gather(1, m2)
    pick_cot(theirs[0])
    forward_b(theirs[0], 0, sx[0].at[0])
    exchanges[0, 0] = start_x(0, 0)
    forward_gu(theirs[0], 1, sx[1].at[0])
    forward_b(theirs[0], 1, sx[1].at[0])
    exchanges[0, 1] = start_x(0, 1)
    pick_rows(mine[0])
    pick_cot(mine[0])
    for h in range(2):
        forward_gu(mine[0], h, own[h].at[0])
        forward_b(mine[0], h, own[h].at[0])
    pick_rows(theirs[1])
    pick_cot(theirs[1])
    for h in range(2):
        forward_gu(theirs[1], h, sx[h].at[1])
        forward_b(theirs[1], h, sx[h].at[1])
        exchanges[1, h] = start_x(1, h)
    pick_rows(mine[1])
    pick_cot(mine[1])
    for h in range(2):
        forward_gu(mine[1], h, own[h].at[1])
        forward_b(mine[1], h, own[h].at[1])

    my_rows = pl.ds(pl.multiple_of(16 * y, 16), 16)
    scatters, spreads, relays = {}, {}, {}

    def reduce_x(p, h):
        exchanges[p, h].wait_recv()
        sy[h][p] = (own[h][p] + rx[h][p].astype(F32)).astype(BF)
        scatters[p, h] = []
        for k in ORDER:
            to = lax.rem(y + k, NY)
            src = sy[h].at[p, pl.ds(pl.multiple_of(16 * to, 16), 16)]
            scatters[p, h].append(
                send(src, ry[h].at[p, k - 1], y_send.at[p, h, k - 1], y_recv.at[p, h, k - 1], y_peer(k))
            )

    def act_grads(gate, up, back):
        c = 0.7978845608028654
        inner = c * (gate + 0.044715 * gate * gate * gate)
        th = jnp.tanh(inner)
        half = 0.5 * (1.0 + th)
        act = gate * half
        slope = half + 0.5 * gate * (1.0 - th * th) * c * (1.0 + 3 * 0.044715 * gate * gate)
        return act * up, back * up * slope, back * act

    def reduce_y(p, h):
        for copy in scatters[p, h]:
            copy.wait_recv()
        total = sy[h][p, my_rows, :].astype(F32)
        for k in range(NY - 1):
            total = total + ry[h][p, k].astype(F32)
        hidden, d_gate, d_up = act_grads(total[:, 0:256], total[:, 256:512], total[:, 512:768])
        parts = [d_gate, d_up, hidden]
        if h == 1:
            both, back = total[:, 768:896], total[:, 896:1024]
            hidden, d_gate, d_up = act_grads(both, pltpu.roll(both, 64, 1), back)
            low = iota((16, 128), 1) < 64
            parts.append(jnp.where(low, d_gate, pltpu.roll(d_up, 64, 1)))
            parts.append(jnp.where(low, hidden, 0.0))
        r = mine[p]
        hb[h][r, my_rows, :] = jnp.concatenate(parts, axis=1).astype(BF)
        block = hb[h].at[r, my_rows]
        spreads[p, h] = [
            send(block, block, ay_send.at[p, h, k - 1], ay_recv.at[p, h, k - 1], y_peer(k)) for k in ORDER
        ]
        relays[p, h] = [send(block, block, ax_send.at[p, h, 0], ax_recv.at[p, h, 0], x_peer)]

    def relay(p, h):
        for k, copy in reversed(list(zip(ORDER, spreads[p, h]))):
            copy.wait_recv()
            source = lax.rem(y + NY - k, NY)
            block = hb[h].at[mine[p], pl.ds(pl.multiple_of(16 * source, 16), 16)]
            relays[p, h].append(send(block, block, ax_send.at[p, h, k], ax_recv.at[p, h, k], x_peer))

    def merge(p, h):
        for copy in relays[p, h]:
            copy.wait_recv()
        cols = slice(256 * h, 256 * h + 256)
        whole = slice(0, 128)
        jobs = [
            (rows_t, slice(0, 256), wg, cols, num_g, den_g, 1.0 / D, og_ref),
            (rows_t, slice(256, 512), wu, cols, num_u, den_u, 1.0 / D, ou_ref),
            (cot_t, slice(512, 768), wd, cols, num_d, den_d, 1.0 / FF, od_ref),
        ]
        if h == 1:
            jobs.append((rows_t, slice(768, 896), wt, whole, num_t, den_t, 1.0 / D, None))
            jobs.append((cot_t, slice(896, 960), wd, slice(512, 576), num_d, den_d, 1.0 / FF, od_ref))
        for left, lanes, weight, cols, num, den, scale, out in jobs:
            n, d = None, None
            for r in (2 * p, 2 * p + 1):
                grad = dot(left[r, 0:DB, :], hb[h][r, :, lanes])
                factor = grad * grad * scale + PRIOR
                term = factor * weight[r, :, cols].astype(F32)
                n, d = (term, factor) if n is None else (n + term, d + factor)
            if p == 0:
                num[:, cols] = n
                den[:, cols] = d
                continue
            merged = ((num[:, cols] + n) / (den[:, cols] + d)).astype(BF)
            if out is None:
                og_ref[:, 512:576] = merged[:, 0:64]
                ou_ref[:, 512:576] = merged[:, 64:128]
            else:
                out[:, cols] = merged

    units = [(0, 0), (0, 1), (1, 0), (1, 1)]
    for slot in range(len(units) + 3):
        for lag, stage in enumerate((reduce_x, reduce_y, relay, merge)):
            if 0 <= slot - lag < len(units):
                stage(*units[slot - lag])

    for copy in sends:
        copy.wait_send()


def on_device(table, token_ids, cotangent, gate_weight, up_weight, down_weight):
    vm = pl.BlockSpec(memory_space=pltpu.VMEM)
    hbm = pl.BlockSpec(memory_space=pl.ANY)
    weight = pltpu.VMEM((RUNS, DB, FB), BF)
    sem = pltpu.SemaphoreType.DMA

    def both(lead, dtype):
        return [pltpu.VMEM(lead + (w,), dtype) for w in WIDTH]

    return pl.pallas_call(
        kernel,
        out_shape=[jax.ShapeDtypeStruct((DB, FB), BF)] * 3,
        in_specs=[pl.BlockSpec(memory_space=pltpu.SMEM), vm, vm, hbm, hbm, hbm],
        out_specs=[vm] * 3,
        scratch_shapes=[
            weight, weight, weight, pltpu.VMEM((RUNS, DB, 128), BF),
            pltpu.VMEM((2, 16, 16, 256), BF), pltpu.VMEM((2, 16, 16, 256), BF),
            pltpu.VMEM((RUNS, TOK, 384), BF), pltpu.VMEM((RUNS, TOK, 384), BF),
            pltpu.VMEM((RUNS, 384, TOK), BF), pltpu.VMEM((RUNS, 384, TOK), BF),
            pltpu.VMEM((256, 384), BF),
            *both((2, TOK), BF), *both((2, TOK), BF), *both((2, TOK), F32), *both((2, TOK), BF),
            *both((2, NY - 1, 16), BF), *both((RUNS, TOK), BF),
            *([pltpu.VMEM((DB, FB), F32)] * 3), pltpu.VMEM((DB, 128), F32),
            *([pltpu.VMEM((DB, FB), F32)] * 3), pltpu.VMEM((DB, 128), F32),
            sem((3,)), sem((2, 15)), sem((2, 15)), sem((2,)), sem((2,)),
            sem((2, 2)), sem((2, 2)), sem((2, 2, 7)), sem((2, 2, 7)),
            sem((2, 2, 7)), sem((2, 2, 7)), sem((2, 2, 8)), sem((2, 2, 8)),
        ],
        compiler_params=pltpu.CompilerParams(
            collective_id=0, has_side_effects=True, vmem_limit_bytes=48 * 1024 * 1024
        ),
        cost_estimate=pl.CostEstimate(flops=1100000000, bytes_accessed=5200000, transcendentals=300000),
    )(token_ids, table, cotangent, gate_weight, up_weight, down_weight)


def solution(mesh):
    return jax.shard_map(
        on_device,
        mesh=mesh,
        in_specs=(
            P("fsdp", "run"),
            P(None, "fsdp"),
            P(None, "fsdp", "run"),
            P(None, "run", "fsdp"),
            P(None, "run", "fsdp"),
            P(None, "run", "fsdp"),
        ),
        out_specs=(P("run", "fsdp"), P("run", "fsdp"), P("run", "fsdp")),
        check_vma=False,
    )
```

time: 299 us -> 93.8 us (0.31)
  waiting for transfers between devices: 146 us -> 0 us
  blocking collectives: 123 us -> 0 us
  Pallas kernels: 0 us -> 83.1 us
  between operations: 14.2 us -> 0.65 us
  matrix products: 10.7 us -> 0 us
  local copies, waits for them, and re-layouts: 3.03 us -> 8.41 us
    psum x1 -> x0, waiting for transfers between devices: 146 us -> none  [on_device(): lax.psum(up_part.astype(jnp.bfloat16), 'run').astype(jnp.float32)]
    all_gather x3 -> x0, blocking collectives: 123 us -> none  [the longest x1 47 us: on_device(): lax.all_gather(table, 'fsdp', axis=0, tiled=True)]
    pallas_call x0 -> x1, Pallas kernels: none -> 83.1 us  [on_device(): pl.pallas_call(kernel, out_shape=[jax.ShapeDtypeStruct((DB, FB), BF)] * 3...]
    dot_general x6 -> x0, matrix products: 10.7 us -> none  [the longest x1 2.87 us: on_device(): jnp.einsum('rtd,rtf->rdf', cot_all, hidden, preferred_element_type=jnp.fl...]
    unnamed x21 -> x15, local copies, waits for them, and re-layouts: 0.87 us -> 8.41 us
  transfers between devices with their start and end apart: 1 -> 0, of which waited for: 1 -> 0; matrix products, arithmetic and copies ran while one was open for 0% -> 0% of each run, Pallas kernels for 0% -> 0%
where the time goes in v1:
time: 93.8 us; the launch traced here: 92.2 us
  Pallas kernels  83.1 us (89%)
  local copies, waits for them, and re-layouts  8.41 us (9%)
    pallas_call x1, Pallas kernels, on_device(): pl.pallas_call(kernel, out_shape=[jax.ShapeDtypeStruct((DB, FB), BF)] * 3...  83.1 us
    unnamed x15, local copies, waits for them, and re-layouts  8.41 us

profile of v1, /device:TPU:6, one launch (start us, length us, event | category | flops | bytes accessed | tf_op | source)
XLA Modules:
  0.0 92.2 jit_solution(1043225039413210823)
XLA Ops:
  0.6 0.0 copy-start
  0.6 1.4 %copy-done = bf16[4,288,576]{2,1,0:T(8,128)(2,1)S(1)} copy-done((bf16[4,288,576]{2,1,0:T(8,128)(2,1)S(1)}, bf16[4,288,576]{2,1,0:T(8,128)(2,1)}, u32[]{:S(2)}) %copy-start) | copy-done | bytes 1327128
  2.0 0.0 copy-start.1
  2.0 1.4 %copy-done.1 = bf16[4,288,576]{2,1,0:T(8,128)(2,1)S(1)} copy-done((bf16[4,288,576]{2,1,0:T(8,128)(2,1)S(1)}, bf16[4,288,576]{2,1,0:T(8,128)(2,1)}, u32[]{:S(2)}) %copy-start.1) | copy-done | bytes 1327128
  3.4 0.0 copy-start.2
  3.4 1.4 %copy-done.2 = bf16[4,288,576]{2,1,0:T(8,128)(2,1)S(1)} copy-done((bf16[4,288,576]{2,1,0:T(8,128)(2,1)S(1)}, bf16[4,288,576]{2,1,0:T(8,128)(2,1)}, u32[]{:S(2)}) %copy-start.2) | copy-done | bytes 1327128
  4.8 0.0 copy-start.3
  4.8 0.7 copy-done.3
  5.5 0.0 copy-start.4
  5.5 0.7 copy-done.4
  6.2 0.0 copy-start.5
  6.2 0.7 copy-done.5
  6.8 83.1 %shard_map.85 = (bf16[288,576]{1,0:T(8,128)(2,1)S(1)}, bf16[288,576]{1,0:T(8,128)(2,1)S(1)}, bf16[288,576]{1,0:T(8,128)(2,1)S(1)}) custom-call(s32[4,4]{1,0:T(4,128)S(1)} %copy-done.5, bf16[8,288]{1,0:T(8,128)(2,1)S(1)} %copy-done.4, bf16[4,4,288]{2,1,0:T(4,128)(2,1)S(1)} %copy-done.3, bf16[4,288,576]{2,1,0:T(8,128)(2,1)S(1)} %copy-done, ...), custom_call_target="tpu_custom_call" | custom-call | flops 1100000000 | bytes 5200000 | tf_op jit(solution)/shard_map/pallas_call | solution.py:292
  89.9 0.7 copy.12
  90.7 0.7 copy.13
  91.4 0.7 copy.14
Async XLA Ops:
  0.6 1.4 %copy-start = (bf16[4,288,576]{2,1,0:T(8,128)(2,1)S(1)}, bf16[4,288,576]{2,1,0:T(8,128)(2,1)}, u32[]{:S(2)}) copy-start(bf16[4,288,576]{2,1,0:T(8,128)(2,1)} %wg_hbm.1) | copy-start | bytes 3981316
  2.0 1.4 %copy-start.1 = (bf16[4,288,576]{2,1,0:T(8,128)(2,1)S(1)}, bf16[4,288,576]{2,1,0:T(8,128)(2,1)}, u32[]{:S(2)}) copy-start(bf16[4,288,576]{2,1,0:T(8,128)(2,1)} %wu_hbm.1) | copy-start | bytes 3981316
  3.4 1.4 %copy-start.2 = (bf16[4,288,576]{2,1,0:T(8,128)(2,1)S(1)}, bf16[4,288,576]{2,1,0:T(8,128)(2,1)}, u32[]{:S(2)}) copy-start(bf16[4,288,576]{2,1,0:T(8,128)(2,1)} %wd_hbm.1) | copy-start | bytes 3981316
  4.8 0.7 copy-start.3
  5.5 0.7 copy-start.4
  6.2 0.7 copy-start.5

commit v2 on v1

--- a/solution.py
+++ b/solution.py
@@ -17,7 +17,8 @@
 BF = jnp.bfloat16
 F32 = jnp.float32
 WIDTH = (768, 1024)
-ORDER = (4, 3, 5, 2, 6, 1, 7)
+GU = (512, 640)
+LAGS = (0.0, 4.0, 8.0, 12.0, 16.0, 20.0)
 
 
 def dot(a, b):
@@ -36,12 +37,13 @@
     ids_ref, table_ref, cot_ref, wg_hbm, wu_hbm, wd_hbm,
     og_ref, ou_ref, od_ref,
     wg, wu, wd, wt, m1, m2, rows_s, cot_s, rows_t, cot_t, tbl,
-    sx0, sx1, rx0, rx1, own0, own1, sy0, sy1, ry0, ry1, h0, h1,
+    sx0, sx1, rx0, rx1, own0, own1, sy0, sy1, ry0, ry1, cy0, cy1, h0, h1,
     num_g, num_u, num_d, num_t, den_g, den_u, den_d, den_t,
     w_sem, g_send, g_recv, f_send, f_recv,
     x_send, x_recv, y_send, y_recv, ay_send, ay_recv, ax_send, ax_recv,
 ):
-    sx, rx, own, sy, ry, hb = (sx0, sx1), (rx0, rx1), (own0, own1), (sy0, sy1), (ry0, ry1), (h0, h1)
+    sx, rx, own, sy = (sx0, sx1), (rx0, rx1), (own0, own1), (sy0, sy1)
+    ry, cy, hb = (ry0, ry1), (cy0, cy1), (h0, h1)
     run, fs = lax.axis_index("run"), lax.axis_index("fsdp")
     y, xl = run // 2, run % 2
     chip, core = fs // 2, fs % 2
@@ -60,7 +62,7 @@
                 gather_peers.append((run, other * 2 + core))
 
     barrier = pltpu.get_barrier_semaphore()
-    everyone = gather_peers + [sibling, x_peer] + [y_peer(k) for k in ORDER]
+    everyone = gather_peers + [sibling, x_peer] + [y_peer(k) for k in (2, 6, 1, 7)]
     for peer in everyone:
         pl.semaphore_signal(barrier, inc=1, device_id=peer, device_id_type=MESH)
 
@@ -147,29 +149,35 @@
         out[:, 0:256] = (dot(rows, wg[r, :, cols]) * D ** -0.5).astype(out.dtype)
         out[:, 256:512] = (dot(rows, wu[r, :, cols]) * D ** -0.5).astype(out.dtype)
         if h == 1:
-            out[:, 768:896] = (dot(rows, wt[r]) * D ** -0.5).astype(out.dtype)
+            out[:, 512:640] = (dot(rows, wt[r]) * D ** -0.5).astype(out.dtype)
 
     def forward_b(r, h, out):
         cots = cot_s[r, :, 0:DB]
-        out[:, 512:768] = (dot(cots, wd[r, :, 256 * h:256 * h + 256]) * FF ** -0.5).astype(out.dtype)
+        out[:, GU[h]:GU[h] + 256] = (dot(cots, wd[r, :, 256 * h:256 * h + 256]) * FF ** -0.5).astype(out.dtype)
         if h == 1:
             last = dot(cots, wd[r, :, 512:576]) * FF ** -0.5
             out[:, 896:1024] = jnp.concatenate([last, jnp.zeros_like(last)], axis=1).astype(out.dtype)
 
-    def start_x(p, h):
-        return send(sx[h].at[p], rx[h].at[p], x_send.at[p, h], x_recv.at[p, h], x_peer)
-
     exchanges = {}
     theirs, mine = (1 - xl, 3 - xl), (xl, 2 + xl)
+
+    def start_x(p, h, part):
+        lanes = (pl.ds(0, GU[h]), pl.ds(GU[h], WIDTH[h] - GU[h]))[part]
+        exchanges[p, h, part] = send(
+            sx[h].at[p, :, lanes], rx[h].at[p, :, lanes], x_send.at[p, h, part], x_recv.at[p, h, part], x_peer
+        )
+
     pick_rows(theirs[0])
     forward_gu(theirs[0], 0, sx[0].at[0])
+    start_x(0, 0, 0)
+    forward_gu(theirs[0], 1, sx[1].at[0])
     finish_gather(1, m2)
     pick_cot(theirs[0])
     forward_b(theirs[0], 0, sx[0].at[0])
-    exchanges[0, 0] = start_x(0, 0)
-    forward_gu(theirs[0], 1, sx[1].at[0])
+    start_x(0, 0, 1)
+    start_x(0, 1, 0)
     forward_b(theirs[0], 1, sx[1].at[0])
-    exchanges[0, 1] = start_x(0, 1)
+    start_x(0, 1, 1)
     pick_rows(mine[0])
     pick_cot(mine[0])
     for h in range(2):
@@ -179,27 +187,45 @@
     pick_cot(theirs[1])
     for h in range(2):
         forward_gu(theirs[1], h, sx[h].at[1])
+        start_x(1, h, 0)
         forward_b(theirs[1], h, sx[h].at[1])
-        exchanges[1, h] = start_x(1, h)
+        start_x(1, h, 1)
     pick_rows(mine[1])
     pick_cot(mine[1])
     for h in range(2):
         forward_gu(mine[1], h, own[h].at[1])
         forward_b(mine[1], h, own[h].at[1])
 
-    my_rows = pl.ds(pl.multiple_of(16 * y, 16), 16)
+    def at(k):
+        return pl.ds(pl.multiple_of(16 * lax.rem(y + NY + k, NY), 16), 16)
+
     scatters, spreads, relays = {}, {}, {}
 
+    def sign(p, h):
+        return 1 if (p + h) % 2 == 0 else -1
+
+    def scatter(p, h, slot, src, to):
+        scatters[p, h, slot] = send(
+            src, ry[h].at[p, slot], y_send.at[p, h, slot], y_recv.at[p, h, slot], y_peer(to % NY)
+        )
+
     def reduce_x(p, h):
-        exchanges[p, h].wait_recv()
+        exchanges[p, h, 0].wait_recv()
+        exchanges[p, h, 1].wait_recv()
         sy[h][p] = (own[h][p] + rx[h][p].astype(F32)).astype(BF)
-        scatters[p, h] = []
-        for k in ORDER:
-            to = lax.rem(y + k, NY)
-            src = sy[h].at[p, pl.ds(pl.multiple_of(16 * to, 16), 16)]
-            scatters[p, h].append(
-                send(src, ry[h].at[p, k - 1], y_send.at[p, h, k - 1], y_recv.at[p, h, k - 1], y_peer(k))
-            )
+        g = sign(p, h)
+        for slot, owner, to in ((0, -4, -2), (1, -3, -1), (2, 3, 1), (3, -1, -1), (4, 1, 1)):
+            scatter(p, h, slot, sy[h].at[p, at(g * owner)], g * to)
+
+    def combine_y(p, h):
+        g = sign(p, h)
+        for i, (slots, owner) in enumerate((((0, 1), -2), ((2,), 2))):
+            total = sy[h][p, at(g * owner), :].astype(F32)
+            for slot in slots:
+                scatters[p, h, slot].wait_recv()
+                total = total + ry[h][p, slot].astype(F32)
+            cy[h][p, i] = total.astype(BF)
+            scatter(p, h, 5 + i, cy[h].at[p, i], g * owner)
 
     def act_grads(gate, up, back):
         c = 0.7978845608028654
@@ -210,34 +236,55 @@
         slope = half + 0.5 * gate * (1.0 - th * th) * c * (1.0 + 3 * 0.044715 * gate * gate)
         return act * up, back * up * slope, back * act
 
-    def reduce_y(p, h):
-        for copy in scatters[p, h]:
-            copy.wait_recv()
-        total = sy[h][p, my_rows, :].astype(F32)
-        for k in range(NY - 1):
-            total = total + ry[h][p, k].astype(F32)
-        hidden, d_gate, d_up = act_grads(total[:, 0:256], total[:, 256:512], total[:, 512:768])
+    def relay(p, h, slot, owner):
+        block = hb[h].at[mine[p], at(owner)]
+        relays[p, h].append(send(block, block, ax_send.at[p, h, slot], ax_recv.at[p, h, slot], x_peer))
+
+    def spread(p, h, slot, owner, to):
+        block = hb[h].at[mine[p], at(owner)]
+        spreads[p, h, slot] = send(
+            block, block, ay_send.at[p, h, slot], ay_recv.at[p, h, slot], y_peer(to % NY)
+        )
+
+    def finish_y(p, h):
+        total = sy[h][p, at(0), :].astype(F32)
+        for slot in (3, 4, 5, 6):
+            scatters[p, h, slot].wait_recv()
+            total = total + ry[h][p, slot].astype(F32)
+        b = GU[h]
+        hidden, d_gate, d_up = act_grads(total[:, 0:256], total[:, 256:512], total[:, b:b + 256])
         parts = [d_gate, d_up, hidden]
         if h == 1:
-            both, back = total[:, 768:896], total[:, 896:1024]
+            both, back = total[:, 512:640], total[:, 896:1024]
             hidden, d_gate, d_up = act_grads(both, pltpu.roll(both, 64, 1), back)
             low = iota((16, 128), 1) < 64
-            parts.append(jnp.where(low, d_gate, pltpu.roll(d_up, 64, 1)))
+            parts.insert(2, jnp.where(low, d_gate, pltpu.roll(d_up, 64, 1)))
             parts.append(jnp.where(low, hidden, 0.0))
-        r = mine[p]
-        hb[h][r, my_rows, :] = jnp.concatenate(parts, axis=1).astype(BF)
-        block = hb[h].at[r, my_rows]
-        spreads[p, h] = [
-            send(block, block, ay_send.at[p, h, k - 1], ay_recv.at[p, h, k - 1], y_peer(k)) for k in ORDER
-        ]
-        relays[p, h] = [send(block, block, ax_send.at[p, h, 0], ax_recv.at[p, h, 0], x_peer)]
-
-    def relay(p, h):
-        for k, copy in reversed(list(zip(ORDER, spreads[p, h]))):
-            copy.wait_recv()
-            source = lax.rem(y + NY - k, NY)
-            block = hb[h].at[mine[p], pl.ds(pl.multiple_of(16 * source, 16), 16)]
-            relays[p, h].append(send(block, block, ax_send.at[p, h, k], ax_recv.at[p, h, k], x_peer))
+        hb[h][mine[p], at(0), :] = jnp.concatenate(parts, axis=1).astype(BF)
+        g = sign(p, h)
+        for slot, to in ((0, 2), (1, -2), (2, 1), (3, -1)):
+            spread(p, h, slot, 0, g * to)
+        relays[p, h] = []
+        relay(p, h, 7, 0)
+
+    def pass_on(p, h):
+        g = sign(p, h)
+        spreads[p, h, 0].wait_recv()
+        spread(p, h, 5, -2 * g, 2 * g)
+        spread(p, h, 4, -2 * g, g)
+        spreads[p, h, 1].wait_recv()
+        spread(p, h, 6, 2 * g, -g)
+        relay(p, h, 0, -2 * g)
+        relay(p, h, 1, 2 * g)
+        for slot, owner in ((2, -1), (3, 1)):
+            spreads[p, h, slot].wait_recv()
+            relay(p, h, slot, g * owner)
+
+    def pass_last(p, h):
+        g = sign(p, h)
+        for slot, owner in ((4, -3), (6, 3), (5, -4)):
+            spreads[p, h, slot].wait_recv()
+            relay(p, h, slot, g * owner)
 
     def merge(p, h):
         for copy in relays[p, h]:
@@ -247,10 +294,10 @@
         jobs = [
             (rows_t, slice(0, 256), wg, cols, num_g, den_g, 1.0 / D, og_ref),
             (rows_t, slice(256, 512), wu, cols, num_u, den_u, 1.0 / D, ou_ref),
-            (cot_t, slice(512, 768), wd, cols, num_d, den_d, 1.0 / FF, od_ref),
+            (cot_t, slice(GU[h], GU[h] + 256), wd, cols, num_d, den_d, 1.0 / FF, od_ref),
         ]
         if h == 1:
-            jobs.append((rows_t, slice(768, 896), wt, whole, num_t, den_t, 1.0 / D, None))
+            jobs.append((rows_t, slice(512, 640), wt, whole, num_t, den_t, 1.0 / D, None))
             jobs.append((cot_t, slice(896, 960), wd, slice(512, 576), num_d, den_d, 1.0 / FF, od_ref))
         for left, lanes, weight, cols, num, den, scale, out in jobs:
             n, d = None, None
@@ -271,13 +318,26 @@
                 out[:, cols] = merged
 
     units = [(0, 0), (0, 1), (1, 0), (1, 1)]
-    for slot in range(len(units) + 3):
-        for lag, stage in enumerate((reduce_x, reduce_y, relay, merge)):
-            if 0 <= slot - lag < len(units):
-                stage(*units[slot - lag])
+    stages = (reduce_x, combine_y, finish_y, pass_on, pass_last, merge)
+    arrival = (4.5, 10.0, 14.0, 19.5)
+    events = [
+        (arrival[i] + lag, i, j)
+        for i in range(len(units))
+        for j, lag in enumerate(LAGS)
+    ]
+    for _, i, j in sorted(events):
+        stages[j](*units[i])
 
     for copy in sends:
         copy.wait_send()
+
+
+def deliver(a, b, c, oa, ob, oc, sems):
+    copies = [pltpu.make_async_copy(s, d, sems.at[i]) for i, (s, d) in enumerate(((a, oa), (b, ob), (c, oc)))]
+    for copy in copies:
+        copy.start()
+    for copy in copies:
+        copy.wait()
 
 
 def on_device(table, token_ids, cotangent, gate_weight, up_weight, down_weight):
@@ -289,7 +349,7 @@
     def both(lead, dtype):
         return [pltpu.VMEM(lead + (w,), dtype) for w in WIDTH]
 
-    return pl.pallas_call(
+    merged = pl.pallas_call(
         kernel,
         out_shape=[jax.ShapeDtypeStruct((DB, FB), BF)] * 3,
         in_specs=[pl.BlockSpec(memory_space=pltpu.SMEM), vm, vm, hbm, hbm, hbm],
@@ -301,18 +361,25 @@
             pltpu.VMEM((RUNS, 384, TOK), BF), pltpu.VMEM((RUNS, 384, TOK), BF),
             pltpu.VMEM((256, 384), BF),
             *both((2, TOK), BF), *both((2, TOK), BF), *both((2, TOK), F32), *both((2, TOK), BF),
-            *both((2, NY - 1, 16), BF), *both((RUNS, TOK), BF),
+            *both((2, NY - 1, 16), BF), *both((2, 2, 16), BF), *both((RUNS, TOK), BF),
             *([pltpu.VMEM((DB, FB), F32)] * 3), pltpu.VMEM((DB, 128), F32),
             *([pltpu.VMEM((DB, FB), F32)] * 3), pltpu.VMEM((DB, 128), F32),
             sem((3,)), sem((2, 15)), sem((2, 15)), sem((2,)), sem((2,)),
-            sem((2, 2)), sem((2, 2)), sem((2, 2, 7)), sem((2, 2, 7)),
+            sem((2, 2, 2)), sem((2, 2, 2)), sem((2, 2, 7)), sem((2, 2, 7)),
             sem((2, 2, 7)), sem((2, 2, 7)), sem((2, 2, 8)), sem((2, 2, 8)),
         ],
         compiler_params=pltpu.CompilerParams(
-            collective_id=0, has_side_effects=True, vmem_limit_bytes=48 * 1024 * 1024
+            collective_id=0, has_side_effects=True, vmem_limit_bytes=60 * 1024 * 1024
         ),
         cost_estimate=pl.CostEstimate(flops=1100000000, bytes_accessed=5200000, transcendentals=300000),
     )(token_ids, table, cotangent, gate_weight, up_weight, down_weight)
+    return pl.pallas_call(
+        deliver,
+        out_shape=[jax.ShapeDtypeStruct((DB, FB), BF)] * 3,
+        in_specs=[vm] * 3,
+        out_specs=[hbm] * 3,
+        scratch_shapes=[pltpu.SemaphoreType.DMA((3,))],
+    )(*merged)
 
 
 def solution(mesh):

time: 93.8 us -> 76.6 us (0.82); the launches traced: 92.2 us -> 76.5 us
  local copies, waits for them, and re-layouts: 8.41 us -> 0 us
  Pallas kernels: 83.1 us -> 75.8 us
    pallas_call x1, Pallas kernels: 83.1 us -> 73.6 us  [on_device(): pl.pallas_call(kernel, out_shape=[jax.ShapeDtypeStruct((DB, FB), BF)] * 3...]
    unnamed x15 -> x0, local copies, waits for them, and re-layouts: 8.41 us -> none
    pallas_call x0 -> x1, Pallas kernels: none -> 2.22 us  [on_device(): pl.pallas_call(deliver, out_shape=[jax.ShapeDtypeStruct((DB, FB), BF)] *...]
where the time goes in v2:
time: 76.6 us; the launch traced here: 76.5 us
  Pallas kernels  75.8 us (99%)
    pallas_call x1, Pallas kernels, on_device(): pl.pallas_call(kernel, out_shape=[jax.ShapeDtypeStruct((DB, FB), BF)] * 3...  73.6 us
    pallas_call x1, Pallas kernels, on_device(): pl.pallas_call(deliver, out_shape=[jax.ShapeDtypeStruct((DB, FB), BF)] *...  2.22 us

profile of v2, /device:TPU:6, one launch (start us, length us, event | category | flops | bytes accessed | tf_op | source)
XLA Modules:
  0.0 76.5 jit_solution(5226414966098304821)
XLA Ops:
  0.6 73.6 %shard_map.85 = (bf16[288,576]{1,0:T(8,128)(2,1)}, bf16[288,576]{1,0:T(8,128)(2,1)}, bf16[288,576]{1,0:T(8,128)(2,1)}) custom-call(s32[4,4]{1,0:T(4,128)} %ids_ref.1, bf16[8,288]{1,0:T(8,128)(2,1)} %table_ref.1, bf16[4,4,288]{2,1,0:T(4,128)(2,1)} %cot_ref.1, bf16[4,288,576]{2,1,0:T(8,128)(2,1)} %wg_hbm.1, bf16[4,288,576]{2,1,0:T(8,128)(2,1)} %wu_hbm.1, ...), custom_call_target="tpu_custom_call" | custom-call | flops 1100000000 | bytes 5200000 | tf_op jit(solution)/shard_map/pallas_call | solution.py:352
  74.2 2.2 %shard_map.86 = (bf16[288,576]{1,0:T(8,128)(2,1)}, bf16[288,576]{1,0:T(8,128)(2,1)}, bf16[288,576]{1,0:T(8,128)(2,1)}) custom-call(bf16[288,576]{1,0:T(8,128)(2,1)} %get-tuple-element.6.a, bf16[288,576]{1,0:T(8,128)(2,1)} %get-tuple-element.7.b, bf16[288,576]{1,0:T(8,128)(2,1)} %get-tuple-element.8.c), custom_call_target="tpu_custom_call" | custom-call | tf_op jit(solution)/shard_map/pallas_call | solution.py:376

commit v3 on v1

v3 whole, which is shorter than its diff:
```python
import jax
import jax.numpy as jnp
from jax import lax
from jax.experimental import pallas as pl
from jax.experimental.pallas import tpu as pltpu
from jax.sharding import PartitionSpec as P

D = 4608
FF = 18432
PRIOR = 0.01
DB = 288
FB = 576
RUNS = 4
TOK = 128
NY = 8
MESH = pl.DeviceIdType.MESH
BF = jnp.bfloat16
F32 = jnp.float32
BLOCKS = ((0, 256, 0), (256, 128, 0), (384, 128, 1))
UNITS = (
    (1, 2, True, False),
    (0, 0, False, False),
    (0, 2, True, False),
    (1, 0, False, False),
    (1, 1, False, False),
    (0, 1, False, True),
)
SIGNS = (-1, 1, 1, -1, -1, 1)
EARLY = (1,)
SCHEDULE = (
    (0, 1), (2, 1), (1, 0), (3, 0), (4, 0), (0, 2), (2, 2), (5, 0), (1, 1), (0, 3),
    (2, 3), (3, 1), (1, 2), (1, 3), (0, 5), (4, 1), (2, 5), (5, 1), (3, 2), (3, 3),
    (1, 5), (0, 6), (4, 2), (4, 3), (5, 2), (5, 3), (2, 6), (3, 5), (1, 6), (4, 5),
    (5, 4), (3, 6), (2, 7), (4, 6), (5, 5), (1, 7), (0, 7), (3, 7), (4, 7), (5, 6),
    (5, 7),
)


def gu_lanes(block):
    return 2 * block[1] + 128 * block[2]


def all_lanes(block):
    return 3 * block[1] + 256 * block[2]


def dot(a, b):
    return jnp.dot(a, b, preferred_element_type=F32)


def iota(shape, dim):
    return lax.broadcasted_iota(jnp.int32, shape, dim)


def place(rows, shift):
    return (iota((rows, 128), 1) == iota((rows, 128), 0) + shift).astype(BF)


def act_grads(gate, up, back):
    c = 0.7978845608028654
    inner = c * (gate + 0.044715 * gate * gate * gate)
    th = jnp.tanh(inner)
    half = 0.5 * (1.0 + th)
    act = gate * half
    slope = half + 0.5 * gate * (1.0 - th * th) * c * (1.0 + 3 * 0.044715 * gate * gate)
    return act * up, back * up * slope, back * act


def kernel(
    ids_ref, table_ref, cot_ref, wg_hbm, wu_hbm, wd_hbm,
    og_ref, ou_ref, od_ref,
    wg, wu, wd, wt, m1, m2, rows_s, cot_s, rows_t, cot_t, tbl,
    num_g, num_u, num_d, num_t, den_g, den_u, den_d, den_t,
    w_sem, g_send, g_recv, f_send, f_recv, x_send, x_recv, y_send, y_recv, c_send, c_recv,
    ay_send, ay_recv, ax_send, ax_recv, *bufs,
):
    n = len(UNITS)
    sx, rx, own, sy, ry, cy, ty, tb, rt, hb = (bufs[n * i:n * i + n] for i in range(10))
    run, fs = lax.axis_index("run"), lax.axis_index("fsdp")
    y, xl = run // 2, run % 2
    chip, core = fs // 2, fs % 2
    xh, z = chip // 8, chip % 8

    def y_peer(k):
        return (lax.rem(y + NY + k, NY) * 2 + xl, fs)

    x_peer = (y * 2 + 1 - xl, fs)
    sibling = (run, chip * 2 + 1 - core)
    gather_peers, gather_chips = [], []
    for dz in (4, 3, 5, 2, 6, 1, 7, 0):
        for dx in (1, 0):
            if dz or dx:
                to = lax.rem(xh + dx, 2) * 8 + lax.rem(z + dz, 8)
                gather_peers.append((run, to * 2 + core))
                gather_chips.append(lax.rem(xh + dx, 2) * 8 + lax.rem(z + 8 - dz, 8))

    barrier = pltpu.get_barrier_semaphore()
    everyone = gather_peers + [sibling, x_peer] + [y_peer(k) for k in (-2, 2, -1, 1)]
    for peer in everyone:
        pl.semaphore_signal(barrier, inc=1, device_id=peer, device_id_type=MESH)

    weight_copies = []
    for i, (src, dst) in enumerate(((wg_hbm, wg), (wu_hbm, wu), (wd_hbm, wd))):
        copy = pltpu.make_async_copy(src, dst, w_sem.at[i])
        copy.start()
        weight_copies.append(copy)

    table = table_ref[...].astype(F32)
    cot = jnp.concatenate([cot_ref[r].astype(F32) for r in range(RUNS)], axis=0)
    ids = jnp.zeros((16, 128), F32)
    row, lane = iota((16, 128), 0), iota((16, 128), 1)
    for r in range(RUNS):
        for t in range(4):
            ids = jnp.where((row == 4 * r + t) & (lane == 64), ids_ref[r, t].astype(F32), ids)
    tail = dot(cot[:, 256:288].astype(BF), place(32, 32))
    table_tail = dot(table[:, 256:288].astype(BF), place(32, 0))
    tail = tail + ids + jnp.concatenate([table_tail, jnp.zeros((8, 128), F32)], axis=0)
    folded = jnp.concatenate([table[:, 0:128], table[:, 128:256]], axis=0)
    m1[core, chip] = jnp.concatenate([folded, tail], axis=1).astype(BF)
    m2[core, chip] = cot[:, 0:256].astype(BF)

    pl.semaphore_wait(barrier, len(everyone))

    sends = []

    def send(src, dst, s_sem, r_sem, peer):
        copy = pltpu.make_async_remote_copy(
            src_ref=src, dst_ref=dst, send_sem=s_sem, recv_sem=r_sem, device_id=peer, device_id_type=MESH
        )
        copy.start()
        sends.append(copy)
        return copy

    def hand_over(j, buf, i, place):
        return send(buf.at[core, place], buf.at[core, place], f_send.at[j, i], f_recv.at[j, i], sibling)

    gathers = []
    for j, buf in enumerate((m1, m2)):
        gathers.append([
            send(buf.at[core, chip], buf.at[core, chip], g_send.at[j, i], g_recv.at[j, i], peer)
            for i, peer in enumerate(gather_peers)
        ])

    for copy in weight_copies:
        copy.wait()
    for r in range(RUNS):
        wt[r] = jnp.concatenate([wg[r, :, 512:576], wu[r, :, 512:576]], axis=1)

    def finish_gather(j, buf):
        handed = [hand_over(j, buf, 15, chip)]
        for i in reversed(range(15)):
            gathers[j][i].wait_recv()
            handed.append(hand_over(j, buf, i, gather_chips[i]))
        for copy in handed:
            copy.wait_recv()

    def picker(r):
        i, g = iota((TOK, 512), 0), iota((TOK, 512), 1)
        return (g == 16 * (i // 4) + 4 * r + i % 4).astype(BF)

    finish_gather(0, m1)
    m1f = m1[...].astype(F32).reshape(32, 16, 256)
    tbl[:, 0:128] = m1f[:, 0:8, 0:128].reshape(256, 128).astype(BF)
    tbl[:, 128:256] = m1f[:, 8:16, 0:128].reshape(256, 128).astype(BF)
    tbl[:, 256:384] = m1f[:, 0:8, 128:256].reshape(256, 128).astype(BF)

    def pick_rows(r):
        z_tail = dot(picker(r), m1[...].reshape(512, 256)[:, 128:256])
        j = iota((TOK, 256), 1)
        entry = ((j % 128) // 8) * 16 + (j // 128) * 8 + j % 8
        hot = (z_tail[:, 64:65].astype(jnp.int32) == entry).astype(BF)
        rows = dot(hot, tbl[...])
        rows_s[r] = rows.astype(BF)
        rows_t[r] = rows.T.astype(BF)
        cot_tail = pltpu.roll(z_tail, 96, 1)
        cot_s[r, :, 256:384] = cot_tail.astype(BF)
        cot_t[r, 256:384, :] = cot_tail.T.astype(BF)

    def pick_cot(r):
        main = dot(picker(r), m2[...].reshape(512, 256))
        cot_s[r, :, 0:256] = main.astype(BF)
        cot_t[r, 0:256, :] = main.T.astype(BF)

    def forward_gu(r, u, out):
        first, w, last = BLOCKS[UNITS[u][1]]
        rows = rows_s[r, :, 0:DB]
        out[:, 0:w] = (dot(rows, wg[r, :, first:first + w]) * D ** -0.5).astype(out.dtype)
        out[:, w:2 * w] = (dot(rows, wu[r, :, first:first + w]) * D ** -0.5).astype(out.dtype)
        if last:
            out[:, 2 * w:2 * w + 128] = (dot(rows, wt[r]) * D ** -0.5).astype(out.dtype)

    def forward_b(r, u, out):
        block = BLOCKS[UNITS[u][1]]
        first, w, last = block
        b = gu_lanes(block)
        cots = cot_s[r, :, 0:DB]
        out[:, b:b + w] = (dot(cots, wd[r, :, first:first + w]) * FF ** -0.5).astype(out.dtype)
        if last:
            left = dot(cots, wd[r, :, 512:576]) * FF ** -0.5
            out[:, b + w:b + w + 128] = jnp.concatenate([left, jnp.zeros_like(left)], axis=1).astype(out.dtype)

    exchanges, scatters, crossings, spreads, relays = {}, {}, {}, {}, {}

    def their_run(u):
        return 2 * UNITS[u][0] + 1 - xl

    def my_run(u):
        return 2 * UNITS[u][0] + xl

    def at(k):
        return pl.ds(pl.multiple_of(16 * lax.rem(y + NY + k, NY), 16), 16)

    def start_x(u, part):
        block = BLOCKS[UNITS[u][1]]
        b = gu_lanes(block)
        lanes = (pl.ds(0, b), pl.ds(b, all_lanes(block) - b))[part]
        exchanges[u, part] = send(
            sx[u].at[:, lanes], rx[u].at[:, lanes], x_send.at[u, part], x_recv.at[u, part], x_peer
        )

    def sign(u):
        return SIGNS[u]

    def scatter(u, slot, src, to):
        scatters[u, slot] = send(src, ry[u].at[slot], y_send.at[u, slot], y_recv.at[u, slot], y_peer(to))

    def scatter_first(u):
        g = sign(u)
        for slot, owner, to in ((0, -4, -2), (1, -3, -1), (2, 3, 1), (3, -1, -1), (4, 1, 1)):
            scatter(u, slot, sy[u].at[:, at(g * owner)], g * to)

    def reduce_x(u):
        if UNITS[u][2]:
            return
        exchanges[u, 0].wait_recv()
        exchanges[u, 1].wait_recv()
        sy[u][0] = (own[u][...] + rx[u][...].astype(F32)).astype(BF)
        scatter_first(u)

    def combine_y(u):
        g = sign(u)
        for i, (slots, owner) in enumerate((((0, 1), -2), ((2,), 2))):
            total = sy[u][:, at(g * owner), :].astype(F32)
            for slot in slots:
                scatters[u, slot].wait_recv()
                total = total + ry[u][slot].astype(F32)
            cy[u][i] = total.astype(BF)
            scatter(u, 5 + i, cy[u].at[i], g * owner)

    def finish_y(u):
        total = sy[u][:, at(0), :].astype(F32)
        for slot in (3, 4, 5, 6):
            scatters[u, slot].wait_recv()
            total = total + ry[u][slot].astype(F32)
        ty[u][...] = total
        if UNITS[u][2]:
            tb[u][...] = total.astype(BF)
            crossings[u] = send(tb[u].at[1 - xl], rt[u], c_send.at[u], c_recv.at[u], x_peer)

    def relay(u, slot, owner):
        block = hb[u].at[xl, at(owner)]
        relays[u].append(send(block, block, ax_send.at[u, slot], ax_recv.at[u, slot], x_peer))

    def spread(u, slot, owner, to):
        block = hb[u].at[:, at(owner)] if UNITS[u][3] else hb[u].at[xl, at(owner)]
        spreads[u, slot] = send(block, block, ay_send.at[u, slot], ay_recv.at[u, slot], y_peer(to))

    def activate(u):
        if UNITS[u][2]:
            crossings[u].wait_recv()
            total = ty[u][xl] + rt[u][...].astype(F32)
        else:
            total = ty[u][0]
        block = BLOCKS[UNITS[u][1]]
        w, b = block[1], gu_lanes(block)
        hidden, d_gate, d_up = act_grads(total[:, 0:w], total[:, w:2 * w], total[:, b:b + w])
        parts = [d_gate, d_up, hidden]
        if block[2]:
            both, back = total[:, 2 * w:2 * w + 128], total[:, b + w:b + w + 128]
            hidden, d_gate, d_up = act_grads(both, pltpu.roll(both, 64, 1), back)
            low = iota((16, 128), 1) < 64
            parts.insert(2, jnp.where(low, d_gate, pltpu.roll(d_up, 64, 1)))
            parts.append(jnp.where(low, hidden, 0.0))
        hb[u][xl, at(0), :] = jnp.concatenate(parts, axis=1).astype(BF)
        relays[u] = []
        if UNITS[u][3]:
            relay(u, 7, 0)
        else:
            spread_first(u)
            relay(u, 7, 0)

    def spread_first(u):
        g = sign(u)
        for slot, to in ((0, 2), (1, -2), (2, 1), (3, -1)):
            spread(u, slot, 0, g * to)

    def cross_back(u):
        if UNITS[u][3]:
            relays[u][0].wait_recv()
            spread_first(u)

    def pass_on(u):
        g = sign(u)
        spreads[u, 0].wait_recv()
        spread(u, 5, -2 * g, 2 * g)
        spread(u, 4, -2 * g, g)
        spreads[u, 1].wait_recv()
        spread(u, 6, 2 * g, -g)
        last = UNITS[u][3]
        if not last:
            relay(u, 0, -2 * g)
            relay(u, 1, 2 * g)
        for slot, owner in ((2, -1), (3, 1)):
            spreads[u, slot].wait_recv()
            if not last:
                relay(u, slot, g * owner)

    def pass_last(u):
        g = sign(u)
        for slot, owner in ((4, -3), (6, 3), (5, -4)):
            spreads[u, slot].wait_recv()
            if not UNITS[u][3]:
                relay(u, slot, g * owner)

    merged_pairs = {}

    def merge(u):
        if not UNITS[u][3]:
            for copy in relays[u]:
                copy.wait_recv()
        p, which = UNITS[u][:2]
        block = BLOCKS[which]
        first, w, last = block
        b = gu_lanes(block)
        cols = slice(first, first + w)
        jobs = [
            (rows_t, slice(0, w), wg, cols, num_g, den_g, 1.0 / D, og_ref),
            (rows_t, slice(w, 2 * w), wu, cols, num_u, den_u, 1.0 / D, ou_ref),
            (cot_t, slice(b, b + w), wd, cols, num_d, den_d, 1.0 / FF, od_ref),
        ]
        if last:
            jobs.append((rows_t, slice(2 * w, 2 * w + 128), wt, slice(0, 128), num_t, den_t, 1.0 / D, None))
            jobs.append((cot_t, slice(b + w, b + w + 64), wd, slice(512, 576), num_d, den_d, 1.0 / FF, od_ref))
        for left, lanes, weight, cols, num, den, scale, out in jobs:
            n, d = None, None
            for i in range(2):
                grad = dot(left[2 * p + i, 0:DB, :], hb[u][i, :, lanes])
                factor = grad * grad * scale + PRIOR
                term = factor * weight[2 * p + i, :, cols].astype(F32)
                n, d = (term, factor) if n is None else (n + term, d + factor)
            if which not in merged_pairs:
                num[:, cols] = n
                den[:, cols] = d
                continue
            merged = ((num[:, cols] + n) / (den[:, cols] + d)).astype(BF)
            if out is None:
                og_ref[:, 512:576] = merged[:, 0:64]
                ou_ref[:, 512:576] = merged[:, 64:128]
            else:
                out[:, cols] = merged
        merged_pairs[which] = True

    have_rows, have_cot, late = set(), set(), []

    def rows_for(key, r):
        if key not in have_rows:
            have_rows.add(key)
            pick_rows(r)

    def cot_for(key, r):
        if key not in have_cot:
            have_cot.add(key)
            pick_cot(r)

    def key_of(u, other):
        return (UNITS[u][0], other)

    def gu_send(u):
        if UNITS[u][2]:
            for i in range(2):
                rows_for(key_of(u, i), 2 * UNITS[u][0] + (xl if i else 1 - xl))
            for i, r in enumerate((their_run(u), my_run(u))):
                forward_gu(r, u, sy[u].at[(1 - xl) if i == 0 else xl])
        else:
            rows_for(key_of(u, 0), their_run(u))
            forward_gu(their_run(u), u, sx[u])
            start_x(u, 0)

    def b_send(u):
        if UNITS[u][2]:
            for i in range(2):
                cot_for(key_of(u, i), 2 * UNITS[u][0] + (xl if i else 1 - xl))
            for i, r in enumerate((their_run(u), my_run(u))):
                forward_b(r, u, sy[u].at[(1 - xl) if i == 0 else xl])
            scatter_first(u)
        else:
            cot_for(key_of(u, 0), their_run(u))
            forward_b(their_run(u), u, sx[u])
            start_x(u, 1)

    def keep(u):
        if not UNITS[u][2]:
            rows_for(key_of(u, 1), my_run(u))
            cot_for(key_of(u, 1), my_run(u))
            forward_gu(my_run(u), u, own[u])
            forward_b(my_run(u), u, own[u])

    for u in EARLY:
        gu_send(u)
    finish_gather(1, m2)
    for u in range(n):
        if u not in EARLY:
            gu_send(u)
        b_send(u)
    for u in range(n):
        keep(u)

    stages = (reduce_x, combine_y, finish_y, activate, cross_back, pass_on, pass_last, merge)
    for u, j in SCHEDULE:
        stages[j](u)

    for copy in sends:
        copy.wait_send()


def deliver(a, b, c, oa, ob, oc, sems):
    copies = [pltpu.make_async_copy(s, d, sems.at[i]) for i, (s, d) in enumerate(((a, oa), (b, ob), (c, oc)))]
    for copy in copies:
        copy.start()
    for copy in copies:
        copy.wait()


def on_device(table, token_ids, cotangent, gate_weight, up_weight, down_weight):
    vm = pl.BlockSpec(memory_space=pltpu.VMEM)
    hbm = pl.BlockSpec(memory_space=pl.ANY)
    weight = pltpu.VMEM((RUNS, DB, FB), BF)
    sem = pltpu.SemaphoreType.DMA
    n = len(UNITS)
    runs = [2 if unit[2] else 1 for unit in UNITS]

    def each(shape_of, dtype):
        return [
            pltpu.VMEM(shape_of(runs[u]) + (all_lanes(BLOCKS[UNITS[u][1]]),), dtype) for u in range(n)
        ]

    merged = pl.pallas_call(
        kernel,
        out_shape=[jax.ShapeDtypeStruct((DB, FB), BF)] * 3,
        in_specs=[pl.BlockSpec(memory_space=pltpu.SMEM), vm, vm, hbm, hbm, hbm],
        out_specs=[vm] * 3,
        scratch_shapes=[
            weight, weight, weight, pltpu.VMEM((RUNS, DB, 128), BF),
            pltpu.VMEM((2, 16, 16, 256), BF), pltpu.VMEM((2, 16, 16, 256), BF),
            pltpu.VMEM((RUNS, TOK, 384), BF), pltpu.VMEM((RUNS, TOK, 384), BF),
            pltpu.VMEM((RUNS, 384, TOK), BF), pltpu.VMEM((RUNS, 384, TOK), BF),
            pltpu.VMEM((256, 384), BF),
            *([pltpu.VMEM((DB, FB), F32)] * 3), pltpu.VMEM((DB, 128), F32),
            *([pltpu.VMEM((DB, FB), F32)] * 3), pltpu.VMEM((DB, 128), F32),
            sem((3,)), sem((2, 15)), sem((2, 15)), sem((2, 16)), sem((2, 16)),
            sem((n, 2)), sem((n, 2)), sem((n, 7)), sem((n, 7)), sem((n,)), sem((n,)),
            sem((n, 7)), sem((n, 7)), sem((n, 8)), sem((n, 8)),
            *each(lambda c: (TOK,), BF), *each(lambda c: (TOK,), BF), *each(lambda c: (TOK,), F32),
            *each(lambda c: (c, TOK), BF), *each(lambda c: (7, c, 16), BF), *each(lambda c: (2, c, 16), BF),
            *each(lambda c: (c, 16), F32), *each(lambda c: (c, 16), BF), *each(lambda c: (16,), BF),
            *each(lambda c: (2, TOK), BF),
        ],
        compiler_params=pltpu.CompilerParams(
            collective_id=0, has_side_effects=True, vmem_limit_bytes=60 * 1024 * 1024
        ),
        cost_estimate=pl.CostEstimate(flops=1100000000, bytes_accessed=5200000, transcendentals=300000),
    )(token_ids, table, cotangent, gate_weight, up_weight, down_weight)
    return pl.pallas_call(
        deliver,
        out_shape=[jax.ShapeDtypeStruct((DB, FB), BF)] * 3,
        in_specs=[vm] * 3,
        out_specs=[hbm] * 3,
        scratch_shapes=[sem((3,))],
    )(*merged)


def solution(mesh):
    return jax.shard_map(
        on_device,
        mesh=mesh,
        in_specs=(
            P("fsdp", "run"),
            P(None, "fsdp"),
            P(None, "fsdp", "run"),
            P(None, "run", "fsdp"),
            P(None, "run", "fsdp"),
            P(None, "run", "fsdp"),
        ),
        out_specs=(P("run", "fsdp"), P("run", "fsdp"), P("run", "fsdp")),
        check_vma=False,
    )
```

time: 93.8 us -> 72.2 us (0.77); the launches traced: 92.2 us -> 71.8 us
  Pallas kernels: 83.1 us -> 71.1 us
  local copies, waits for them, and re-layouts: 8.41 us -> 0 us
    pallas_call x1, Pallas kernels: 83.1 us -> 68.9 us  [on_device(): pl.pallas_call(kernel, out_shape=[jax.ShapeDtypeStruct((DB, FB), BF)] * 3...]
    unnamed x15 -> x0, local copies, waits for them, and re-layouts: 8.41 us -> none
    pallas_call x0 -> x1, Pallas kernels: none -> 2.22 us  [on_device(): pl.pallas_call(deliver, out_shape=[jax.ShapeDtypeStruct((DB, FB), BF)] *...]
where the time goes in v3:
time: 72.2 us; the launch traced here: 71.8 us
  Pallas kernels  71.1 us (98%)
    pallas_call x1, Pallas kernels, on_device(): pl.pallas_call(kernel, out_shape=[jax.ShapeDtypeStruct((DB, FB), BF)] * 3...  68.9 us
    pallas_call x1, Pallas kernels, on_device(): pl.pallas_call(deliver, out_shape=[jax.ShapeDtypeStruct((DB, FB), BF)] *...  2.22 us

profile of v3, /device:TPU:6, one launch (start us, length us, event | category | flops | bytes accessed | tf_op | source)
XLA Modules:
  0.0 71.8 jit_solution(12354816245760804726)
XLA Ops:
  0.6 68.9 %shard_map.85 = (bf16[288,576]{1,0:T(8,128)(2,1)}, bf16[288,576]{1,0:T(8,128)(2,1)}, bf16[288,576]{1,0:T(8,128)(2,1)}) custom-call(s32[4,4]{1,0:T(4,128)} %ids_ref.1, bf16[8,288]{1,0:T(8,128)(2,1)} %table_ref.1, bf16[4,4,288]{2,1,0:T(4,128)(2,1)} %cot_ref.1, bf16[4,288,576]{2,1,0:T(8,128)(2,1)} %wg_hbm.1, bf16[4,288,576]{2,1,0:T(8,128)(2,1)} %wu_hbm.1, ...), custom_call_target="tpu_custom_call" | custom-call | flops 1100000000 | bytes 5200000 | tf_op jit(solution)/shard_map/pallas_call | solution.py:447
  69.5 2.2 %shard_map.86 = (bf16[288,576]{1,0:T(8,128)(2,1)}, bf16[288,576]{1,0:T(8,128)(2,1)}, bf16[288,576]{1,0:T(8,128)(2,1)}) custom-call(bf16[288,576]{1,0:T(8,128)(2,1)} %get-tuple-element.6.a, bf16[288,576]{1,0:T(8,128)(2,1)} %get-tuple-element.7.b, bf16[288,576]{1,0:T(8,128)(2,1)} %get-tuple-element.8.c), custom_call_target="tpu_custom_call" | custom-call | tf_op jit(solution)/shard_map/pallas_call | solution.py:473

commit v4 on v3

--- a/solution.py
+++ b/solution.py
@@ -18,21 +18,21 @@
 F32 = jnp.float32
 BLOCKS = ((0, 256, 0), (256, 128, 0), (384, 128, 1))
 UNITS = (
-    (1, 2, True, False),
-    (0, 0, False, False),
-    (0, 2, True, False),
-    (1, 0, False, False),
-    (1, 1, False, False),
-    (0, 1, False, True),
+    (1, 1, True, True, True, True),
+    (1, 0, False, False, False, False),
+    (0, 2, True, True, True, True),
+    (1, 2, True, True, True, True),
+    (0, 1, False, False, False, False),
+    (0, 0, False, False, False, False),
 )
-SIGNS = (-1, 1, 1, -1, -1, 1)
+SIGNS = (1, -1, 1, -1, 1, -1)
 EARLY = (1,)
 SCHEDULE = (
-    (0, 1), (2, 1), (1, 0), (3, 0), (4, 0), (0, 2), (2, 2), (5, 0), (1, 1), (0, 3),
-    (2, 3), (3, 1), (1, 2), (1, 3), (0, 5), (4, 1), (2, 5), (5, 1), (3, 2), (3, 3),
-    (1, 5), (0, 6), (4, 2), (4, 3), (5, 2), (5, 3), (2, 6), (3, 5), (1, 6), (4, 5),
-    (5, 4), (3, 6), (2, 7), (4, 6), (5, 5), (1, 7), (0, 7), (3, 7), (4, 7), (5, 6),
-    (5, 7),
+    (0, 1), (1, 0), (2, 1), (4, 0), (0, 2), (3, 1), (2, 2), (1, 1), (0, 3), (3, 2),
+    (4, 1), (2, 3), (5, 0), (0, 4), (1, 3), (1, 4), (3, 3), (4, 3), (4, 4), (2, 4),
+    (0, 5), (5, 1), (3, 4), (1, 6), (2, 5), (4, 6), (3, 5), (0, 6), (5, 3), (5, 4),
+    (2, 6), (3, 6), (1, 8), (0, 7), (5, 6), (2, 7), (4, 8), (3, 7), (1, 9), (0, 8),
+    (5, 8), (0, 9), (4, 9), (2, 8), (2, 9), (3, 8), (3, 9), (5, 9),
 )
 
 
@@ -67,9 +67,9 @@
 
 
 def kernel(
-    ids_ref, table_ref, cot_ref, wg_hbm, wu_hbm, wd_hbm,
+    ids_hbm, table_hbm, cot_hbm, wg_hbm, wu_hbm, wd_hbm,
     og_ref, ou_ref, od_ref,
-    wg, wu, wd, wt, m1, m2, rows_s, cot_s, rows_t, cot_t, tbl,
+    ids_ref, table_ref, cot_ref, wg, wu, wd, wt, m1, m2, rows_s, cot_s, rows_t, cot_t, tbl,
     num_g, num_u, num_d, num_t, den_g, den_u, den_d, den_t,
     w_sem, g_send, g_recv, f_send, f_recv, x_send, x_recv, y_send, y_recv, c_send, c_recv,
     ay_send, ay_recv, ax_send, ax_recv, *bufs,
@@ -99,12 +99,19 @@
     for peer in everyone:
         pl.semaphore_signal(barrier, inc=1, device_id=peer, device_id_type=MESH)
 
+    small_copies = []
+    for i, (src, dst) in enumerate(((ids_hbm, ids_ref), (table_hbm, table_ref), (cot_hbm, cot_ref))):
+        copy = pltpu.make_async_copy(src, dst, w_sem.at[3 + i])
+        copy.start()
+        small_copies.append(copy)
     weight_copies = []
     for i, (src, dst) in enumerate(((wg_hbm, wg), (wu_hbm, wu), (wd_hbm, wd))):
         copy = pltpu.make_async_copy(src, dst, w_sem.at[i])
         copy.start()
         weight_copies.append(copy)
 
+    for copy in small_copies:
+        copy.wait()
     table = table_ref[...].astype(F32)
     cot = jnp.concatenate([cot_ref[r].astype(F32) for r in range(RUNS)], axis=0)
     ids = jnp.zeros((16, 128), F32)
@@ -226,7 +233,8 @@
 
     def scatter_first(u):
         g = sign(u)
-        for slot, owner, to in ((0, -4, -2), (1, -3, -1), (2, 3, 1), (3, -1, -1), (4, 1, 1)):
+        direct = () if UNITS[u][3] else ((3, -1, -1), (4, 1, 1))
+        for slot, owner, to in ((0, -4, -2), (1, -3, -1), (2, 3, 1)) + direct:
             scatter(u, slot, sy[u].at[:, at(g * owner)], g * to)
 
     def reduce_x(u):
@@ -237,21 +245,29 @@
         sy[u][0] = (own[u][...] + rx[u][...].astype(F32)).astype(BF)
         scatter_first(u)
 
+    def add_arrived(u, owner, slots):
+        total = sy[u][:, at(owner), :].astype(F32)
+        for slot in slots:
+            scatters[u, slot].wait_recv()
+            total = total + ry[u][slot].astype(F32)
+        return total
+
     def combine_y(u):
         g = sign(u)
-        for i, (slots, owner) in enumerate((((0, 1), -2), ((2,), 2))):
-            total = sy[u][:, at(g * owner), :].astype(F32)
-            for slot in slots:
-                scatters[u, slot].wait_recv()
-                total = total + ry[u][slot].astype(F32)
-            cy[u][i] = total.astype(BF)
-            scatter(u, 5 + i, cy[u].at[i], g * owner)
+        step, sent = (1, 3) if UNITS[u][3] else (2, 5)
+        for i, (slots, side) in enumerate((((0, 1), -1), ((2,), 1))):
+            cy[u][i] = add_arrived(u, 2 * side * g, slots).astype(BF)
+            scatter(u, sent + i, cy[u].at[i], g * side * step)
+
+    def combine_again(u):
+        if UNITS[u][3]:
+            g = sign(u)
+            for i, side in enumerate((-1, 1)):
+                cy[u][2 + i] = add_arrived(u, side * g, (3 + i,)).astype(BF)
+                scatter(u, 5 + i, cy[u].at[2 + i], g * side)
 
     def finish_y(u):
-        total = sy[u][:, at(0), :].astype(F32)
-        for slot in (3, 4, 5, 6):
-            scatters[u, slot].wait_recv()
-            total = total + ry[u][slot].astype(F32)
+        total = add_arrived(u, 0, (5, 6) if UNITS[u][3] else (3, 4, 5, 6))
         ty[u][...] = total
         if UNITS[u][2]:
             tb[u][...] = total.astype(BF)
@@ -262,7 +278,7 @@
         relays[u].append(send(block, block, ax_send.at[u, slot], ax_recv.at[u, slot], x_peer))
 
     def spread(u, slot, owner, to):
-        block = hb[u].at[:, at(owner)] if UNITS[u][3] else hb[u].at[xl, at(owner)]
+        block = hb[u].at[:, at(owner)] if UNITS[u][4] else hb[u].at[xl, at(owner)]
         spreads[u, slot] = send(block, block, ay_send.at[u, slot], ay_recv.at[u, slot], y_peer(to))
 
     def activate(u):
@@ -283,7 +299,7 @@
             parts.append(jnp.where(low, hidden, 0.0))
         hb[u][xl, at(0), :] = jnp.concatenate(parts, axis=1).astype(BF)
         relays[u] = []
-        if UNITS[u][3]:
+        if UNITS[u][4]:
             relay(u, 7, 0)
         else:
             spread_first(u)
@@ -291,41 +307,57 @@
 
     def spread_first(u):
         g = sign(u)
-        for slot, to in ((0, 2), (1, -2), (2, 1), (3, -1)):
+        for slot, to in ((0, 1), (1, -1)) if UNITS[u][5] else ((0, 2), (1, -2), (2, 1), (3, -1)):
             spread(u, slot, 0, g * to)
 
     def cross_back(u):
-        if UNITS[u][3]:
+        if UNITS[u][4]:
             relays[u][0].wait_recv()
             spread_first(u)
 
+    def arrived(u, slot, owner):
+        spreads[u, slot].wait_recv()
+        if not UNITS[u][4]:
+            relay(u, slot, owner)
+
+    def pass_far(u, first, second):
+        g = sign(u)
+        spreads[u, first].wait_recv()
+        spread(u, 5, -2 * g, 2 * g)
+        spread(u, 4, -2 * g, g)
+        spreads[u, second].wait_recv()
+        spread(u, 6, 2 * g, -g)
+        if not UNITS[u][4]:
+            relay(u, first, -2 * g)
+            relay(u, second, 2 * g)
+
     def pass_on(u):
         g = sign(u)
-        spreads[u, 0].wait_recv()
-        spread(u, 5, -2 * g, 2 * g)
-        spread(u, 4, -2 * g, g)
-        spreads[u, 1].wait_recv()
-        spread(u, 6, 2 * g, -g)
-        last = UNITS[u][3]
-        if not last:
-            relay(u, 0, -2 * g)
-            relay(u, 1, 2 * g)
-        for slot, owner in ((2, -1), (3, 1)):
-            spreads[u, slot].wait_recv()
-            if not last:
-                relay(u, slot, g * owner)
+        if UNITS[u][5]:
+            for slot, side in ((0, 1), (1, -1)):
+                spreads[u, slot].wait_recv()
+                spread(u, 2 + slot, -side * g, side * g)
+            if not UNITS[u][4]:
+                relay(u, 0, -g)
+                relay(u, 1, g)
+        else:
+            pass_far(u, 0, 1)
+            arrived(u, 2, -g)
+            arrived(u, 3, g)
+
+    def pass_again(u):
+        if UNITS[u][5]:
+            pass_far(u, 2, 3)
 
     def pass_last(u):
         g = sign(u)
         for slot, owner in ((4, -3), (6, 3), (5, -4)):
-            spreads[u, slot].wait_recv()
-            if not UNITS[u][3]:
-                relay(u, slot, g * owner)
+            arrived(u, slot, g * owner)
 
     merged_pairs = {}
 
     def merge(u):
-        if not UNITS[u][3]:
+        if not UNITS[u][4]:
             for copy in relays[u]:
                 copy.wait_recv()
         p, which = UNITS[u][:2]
@@ -415,7 +447,9 @@
     for u in range(n):
         keep(u)
 
-    stages = (reduce_x, combine_y, finish_y, activate, cross_back, pass_on, pass_last, merge)
+    stages = (
+        reduce_x, combine_y, combine_again, finish_y, activate, cross_back, pass_on, pass_again, pass_last, merge,
+    )
     for u, j in SCHEDULE:
         stages[j](u)
 
@@ -423,12 +457,22 @@
         copy.wait_send()
 
 
-def deliver(a, b, c, oa, ob, oc, sems):
-    copies = [pltpu.make_async_copy(s, d, sems.at[i]) for i, (s, d) in enumerate(((a, oa), (b, ob), (c, oc)))]
-    for copy in copies:
-        copy.start()
-    for copy in copies:
-        copy.wait()
+def deliver(a, b, c, oa, ob, oc, held, in_sems, out_sems):
+    parts = [(i, j, s, d) for j in range(2) for i, (s, d) in enumerate(((a, oa), (b, ob), (c, oc)))]
+    copies = []
+    for i, j, s, d in parts:
+        rows = pl.ds(144 * j, 144)
+        copies.append((
+            pltpu.make_async_copy(s.at[rows], held.at[i, rows], in_sems.at[i, j]),
+            pltpu.make_async_copy(held.at[i, rows], d.at[rows], out_sems.at[i, j]),
+        ))
+    for inward, _ in copies:
+        inward.start()
+    for inward, outward in copies:
+        inward.wait()
+        outward.start()
+    for _, outward in copies:
+        outward.wait()
 
 
 def on_device(table, token_ids, cotangent, gate_weight, up_weight, down_weight):
@@ -447,9 +491,10 @@
     merged = pl.pallas_call(
         kernel,
         out_shape=[jax.ShapeDtypeStruct((DB, FB), BF)] * 3,
-        in_specs=[pl.BlockSpec(memory_space=pltpu.SMEM), vm, vm, hbm, hbm, hbm],
+        in_specs=[hbm] * 6,
         out_specs=[vm] * 3,
         scratch_shapes=[
+            pltpu.SMEM((RUNS, 4), jnp.int32), pltpu.VMEM((8, DB), BF), pltpu.VMEM((RUNS, 4, DB), BF),
             weight, weight, weight, pltpu.VMEM((RUNS, DB, 128), BF),
             pltpu.VMEM((2, 16, 16, 256), BF), pltpu.VMEM((2, 16, 16, 256), BF),
             pltpu.VMEM((RUNS, TOK, 384), BF), pltpu.VMEM((RUNS, TOK, 384), BF),
@@ -457,25 +502,25 @@
             pltpu.VMEM((256, 384), BF),
             *([pltpu.VMEM((DB, FB), F32)] * 3), pltpu.VMEM((DB, 128), F32),
             *([pltpu.VMEM((DB, FB), F32)] * 3), pltpu.VMEM((DB, 128), F32),
-            sem((3,)), sem((2, 15)), sem((2, 15)), sem((2, 16)), sem((2, 16)),
+            sem((6,)), sem((2, 15)), sem((2, 15)), sem((2, 16)), sem((2, 16)),
             sem((n, 2)), sem((n, 2)), sem((n, 7)), sem((n, 7)), sem((n,)), sem((n,)),
             sem((n, 7)), sem((n, 7)), sem((n, 8)), sem((n, 8)),
             *each(lambda c: (TOK,), BF), *each(lambda c: (TOK,), BF), *each(lambda c: (TOK,), F32),
-            *each(lambda c: (c, TOK), BF), *each(lambda c: (7, c, 16), BF), *each(lambda c: (2, c, 16), BF),
+            *each(lambda c: (c, TOK), BF), *each(lambda c: (7, c, 16), BF), *each(lambda c: (4, c, 16), BF),
             *each(lambda c: (c, 16), F32), *each(lambda c: (c, 16), BF), *each(lambda c: (16,), BF),
             *each(lambda c: (2, TOK), BF),
         ],
         compiler_params=pltpu.CompilerParams(
-            collective_id=0, has_side_effects=True, vmem_limit_bytes=60 * 1024 * 1024
+            collective_id=0, has_side_effects=True, vmem_limit_bytes=62 * 1024 * 1024
         ),
         cost_estimate=pl.CostEstimate(flops=1100000000, bytes_accessed=5200000, transcendentals=300000),
     )(token_ids, table, cotangent, gate_weight, up_weight, down_weight)
     return pl.pallas_call(
         deliver,
         out_shape=[jax.ShapeDtypeStruct((DB, FB), BF)] * 3,
-        in_specs=[vm] * 3,
+        in_specs=[hbm] * 3,
         out_specs=[hbm] * 3,
-        scratch_shapes=[sem((3,))],
+        scratch_shapes=[pltpu.VMEM((3, DB, FB), BF), sem((3, 2)), sem((3, 2))],
     )(*merged)
 
 

time: 72.2 us -> 70 us (0.970)
  Pallas kernels: 71.1 us -> 68.9 us
    pallas_call x1, Pallas kernels: 68.9 us -> 66.8 us  [on_device(): pl.pallas_call(kernel, out_shape=[jax.ShapeDtypeStruct((DB, FB), BF)] * 3...]
where the time goes in v4:
time: 70 us; the launch traced here: 69.5 us
  Pallas kernels  68.9 us (98%)
    pallas_call x1, Pallas kernels, on_device(): pl.pallas_call(kernel, out_shape=[jax.ShapeDtypeStruct((DB, FB), BF)] * 3...  66.8 us
    pallas_call x1, Pallas kernels, on_device(): pl.pallas_call(deliver, out_shape=[jax.ShapeDtypeStruct((DB, FB), BF)] *...  2.1 us

profile of v4, /device:TPU:6, one launch (start us, length us, event | category | flops | bytes accessed | tf_op | source)
XLA Modules:
  0.0 69.5 jit_solution(5519543295376715307)
XLA Ops:
  0.6 66.8 %shard_map.85 = (bf16[288,576]{1,0:T(8,128)(2,1)}, bf16[288,576]{1,0:T(8,128)(2,1)}, bf16[288,576]{1,0:T(8,128)(2,1)}) custom-call(s32[4,4]{1,0:T(4,128)} %ids_hbm.1, bf16[8,288]{1,0:T(8,128)(2,1)} %table_hbm.1, bf16[4,4,288]{2,1,0:T(4,128)(2,1)} %cot_hbm.1, bf16[4,288,576]{2,1,0:T(8,128)(2,1)} %wg_hbm.1, bf16[4,288,576]{2,1,0:T(8,128)(2,1)} %wu_hbm.1, ...), custom_call_target="tpu_custom_call" | custom-call | flops 1100000000 | bytes 5200000 | tf_op jit(solution)/shard_map/pallas_call | solution.py:491
  67.4 2.1 %shard_map.86 = (bf16[288,576]{1,0:T(8,128)(2,1)}, bf16[288,576]{1,0:T(8,128)(2,1)}, bf16[288,576]{1,0:T(8,128)(2,1)}) custom-call(bf16[288,576]{1,0:T(8,128)(2,1)} %get-tuple-element.6.a, bf16[288,576]{1,0:T(8,128)(2,1)} %get-tuple-element.7.b, bf16[288,576]{1,0:T(8,128)(2,1)} %get-tuple-element.8.c), custom_call_target="tpu_custom_call" | custom-call | tf_op jit(solution)/shard_map/pallas_call | solution.py:518

commit v5 on v4

--- a/solution.py
+++ b/solution.py
@@ -28,10 +28,10 @@
 SIGNS = (1, -1, 1, -1, 1, -1)
 EARLY = (1,)
 SCHEDULE = (
-    (0, 1), (1, 0), (2, 1), (4, 0), (0, 2), (3, 1), (2, 2), (1, 1), (0, 3), (3, 2),
-    (4, 1), (2, 3), (5, 0), (0, 4), (1, 3), (1, 4), (3, 3), (4, 3), (4, 4), (2, 4),
+    (0, 1), (1, 0), (2, 1), (4, 0), (0, 2), (3, 1), (1, 1), (2, 2), (4, 1), (0, 3),
+    (3, 2), (5, 0), (1, 3), (2, 3), (0, 4), (1, 4), (3, 3), (4, 3), (4, 4), (2, 4),
     (0, 5), (5, 1), (3, 4), (1, 6), (2, 5), (4, 6), (3, 5), (0, 6), (5, 3), (5, 4),
-    (2, 6), (3, 6), (1, 8), (0, 7), (5, 6), (2, 7), (4, 8), (3, 7), (1, 9), (0, 8),
+    (1, 8), (2, 6), (3, 6), (0, 7), (5, 6), (2, 7), (4, 8), (3, 7), (1, 9), (0, 8),
     (5, 8), (0, 9), (4, 9), (2, 8), (2, 9), (3, 8), (3, 9), (5, 9),
 )
 
@@ -154,6 +154,11 @@
         wt[r] = jnp.concatenate([wg[r, :, 512:576], wu[r, :, 512:576]], axis=1)
 
     def finish_gather(j, buf):
+        if j == 1:
+            for copy in gathers[j]:
+                copy.wait_recv()
+            send(buf.at[core], buf.at[core], f_send.at[j, 0], f_recv.at[j, 0], sibling).wait_recv()
+            return
         handed = [hand_over(j, buf, 15, chip)]
         for i in reversed(range(15)):
             gathers[j][i].wait_recv()
@@ -440,20 +445,28 @@
     for u in EARLY:
         gu_send(u)
     finish_gather(1, m2)
+    for u in EARLY:
+        b_send(u)
     for u in range(n):
         if u not in EARLY:
             gu_send(u)
-        b_send(u)
+            b_send(u)
     for u in range(n):
         keep(u)
 
     stages = (
         reduce_x, combine_y, combine_again, finish_y, activate, cross_back, pass_on, pass_again, pass_last, merge,
     )
-    for u, j in SCHEDULE:
+    issued, waited = [], 0
+    for step, (u, j) in enumerate(SCHEDULE):
+        issued.append(len(sends))
+        if step >= 8:
+            for copy in sends[waited:issued[step - 8]]:
+                copy.wait_send()
+            waited = issued[step - 8]
         stages[j](u)
 
-    for copy in sends:
+    for copy in sends[waited:]:
         copy.wait_send()
 
 

time: 70 us -> 69.2 us (0.989)
  Pallas kernels: 68.9 us -> 68 us
    pallas_call x1, Pallas kernels: 66.8 us -> 65.9 us  [on_device(): pl.pallas_call(kernel, out_shape=[jax.ShapeDtypeStruct((DB, FB), BF)] * 3...]
where the time goes in v5:
time: 69.2 us; the launch traced here: 68.6 us
  Pallas kernels  68 us (98%)
    pallas_call x1, Pallas kernels, on_device(): pl.pallas_call(kernel, out_shape=[jax.ShapeDtypeStruct((DB, FB), BF)] * 3...  65.9 us
    pallas_call x1, Pallas kernels, on_device(): pl.pallas_call(deliver, out_shape=[jax.ShapeDtypeStruct((DB, FB), BF)] *...  2.1 us

profile of v5, /device:TPU:6, one launch (start us, length us, event | category | flops | bytes accessed | tf_op | source)
XLA Modules:
  0.0 68.6 jit_solution(2033977215265556071)
XLA Ops:
  0.6 65.9 %shard_map.85 = (bf16[288,576]{1,0:T(8,128)(2,1)}, bf16[288,576]{1,0:T(8,128)(2,1)}, bf16[288,576]{1,0:T(8,128)(2,1)}) custom-call(s32[4,4]{1,0:T(4,128)} %ids_hbm.1, bf16[8,288]{1,0:T(8,128)(2,1)} %table_hbm.1, bf16[4,4,288]{2,1,0:T(4,128)(2,1)} %cot_hbm.1, bf16[4,288,576]{2,1,0:T(8,128)(2,1)} %wg_hbm.1, bf16[4,288,576]{2,1,0:T(8,128)(2,1)} %wu_hbm.1, ...), custom_call_target="tpu_custom_call" | custom-call | flops 1100000000 | bytes 5200000 | tf_op jit(solution)/shard_map/pallas_call | solution.py:504
  66.5 2.1 %shard_map.86 = (bf16[288,576]{1,0:T(8,128)(2,1)}, bf16[288,576]{1,0:T(8,128)(2,1)}, bf16[288,576]{1,0:T(8,128)(2,1)}) custom-call(bf16[288,576]{1,0:T(8,128)(2,1)} %get-tuple-element.6.a, bf16[288,576]{1,0:T(8,128)(2,1)} %get-tuple-element.7.b, bf16[288,576]{1,0:T(8,128)(2,1)} %get-tuple-element.8.c), custom_call_target="tpu_custom_call" | custom-call | tf_op jit(solution)/shard_map/pallas_call | solution.py:531

commit v6 on v5

--- a/solution.py
+++ b/solution.py
@@ -183,15 +183,12 @@
         hot = (z_tail[:, 64:65].astype(jnp.int32) == entry).astype(BF)
         rows = dot(hot, tbl[...])
         rows_s[r] = rows.astype(BF)
-        rows_t[r] = rows.T.astype(BF)
         cot_tail = pltpu.roll(z_tail, 96, 1)
         cot_s[r, :, 256:384] = cot_tail.astype(BF)
-        cot_t[r, 256:384, :] = cot_tail.T.astype(BF)
 
     def pick_cot(r):
         main = dot(picker(r), m2[...].reshape(512, 256))
         cot_s[r, :, 0:256] = main.astype(BF)
-        cot_t[r, 0:256, :] = main.T.astype(BF)
 
     def forward_gu(r, u, out):
         first, w, last = BLOCKS[UNITS[u][1]]
@@ -453,6 +450,9 @@
             b_send(u)
     for u in range(n):
         keep(u)
+    for r in range(RUNS):
+        rows_t[r] = rows_s[r].astype(F32).T.astype(BF)
+        cot_t[r] = cot_s[r].astype(F32).T.astype(BF)
 
     stages = (
         reduce_x, combine_y, combine_again, finish_y, activate, cross_back, pass_on, pass_again, pass_last, merge,

time: 69.2 us -> 69.2 us (level)
  no operation moved by 1% of the time
where the time goes in v6:
time: 69.2 us; the launch traced here: 68.7 us
  Pallas kernels  68 us (98%)
    pallas_call x1, Pallas kernels, on_device(): pl.pallas_call(kernel, out_shape=[jax.ShapeDtypeStruct((DB, FB), BF)] * 3...  65.9 us
    pallas_call x1, Pallas kernels, on_device(): pl.pallas_call(deliver, out_shape=[jax.ShapeDtypeStruct((DB, FB), BF)] *...  2.1 us

profile of v6, /device:TPU:6, one launch (start us, length us, event | category | flops | bytes accessed | tf_op | source)
XLA Modules:
  0.0 68.7 jit_solution(3682332983875086179)
XLA Ops:
  0.6 65.9 %shard_map.85 = (bf16[288,576]{1,0:T(8,128)(2,1)}, bf16[288,576]{1,0:T(8,128)(2,1)}, bf16[288,576]{1,0:T(8,128)(2,1)}) custom-call(s32[4,4]{1,0:T(4,128)} %ids_hbm.1, bf16[8,288]{1,0:T(8,128)(2,1)} %table_hbm.1, bf16[4,4,288]{2,1,0:T(4,128)(2,1)} %cot_hbm.1, bf16[4,288,576]{2,1,0:T(8,128)(2,1)} %wg_hbm.1, bf16[4,288,576]{2,1,0:T(8,128)(2,1)} %wu_hbm.1, ...), custom_call_target="tpu_custom_call" | custom-call | flops 1100000000 | bytes 5200000 | tf_op jit(solution)/shard_map/pallas_call | solution.py:504
  66.6 2.1 %shard_map.86 = (bf16[288,576]{1,0:T(8,128)(2,1)}, bf16[288,576]{1,0:T(8,128)(2,1)}, bf16[288,576]{1,0:T(8,128)(2,1)}) custom-call(bf16[288,576]{1,0:T(8,128)(2,1)} %get-tuple-element.6.a, bf16[288,576]{1,0:T(8,128)(2,1)} %get-tuple-element.7.b, bf16[288,576]{1,0:T(8,128)(2,1)} %get-tuple-element.8.c), custom_call_target="tpu_custom_call" | custom-call | tf_op jit(solution)/shard_map/pallas_call | solution.py:531
